TPU v7x, 128 devices: a whole 4x4x4 slice. The times are simulated.
128 devices in a mesh: dp: 16 (over x, y), tensor: 8 (over z, core).
Axes of the slice: x: 4, y: 4, z: 4, core: 2. Of those that a mesh axis runs over, the one named last changes fastest.
Arguments:
- inputs: bfloat16 [16384, 2048], P('dp'), may hold values from -6 to 6
- doc_lengths: int32 [16, 4], P('dp'), may hold values from 1 to 512, 1024 in all within a row
- norm1_gain: float32 [2048], replicated, may hold values from 0.5 to 1.5
- w_query: bfloat16 [2048, 2048], P(None, 'tensor'), may hold values from -0.125 to 0.125
- w_shared_kv: bfloat16 [2048, 256], replicated, may hold values from -0.125 to 0.125
- w_output: bfloat16 [2048, 2048], P('tensor'), may hold values from -1.5 to 1.5
- norm2_gain: float32 [2048], replicated, may hold values from 0.5 to 1.5
- w_gate: bfloat16 [2048, 5632], P(None, 'tensor'), may hold values from -0.125 to 0.125
- w_up: bfloat16 [2048, 5632], P(None, 'tensor'), may hold values from -0.125 to 0.125
- w_down: bfloat16 [5632, 2048], P('tensor'), may hold values from -0.078125 to 0.078125
- out_cotangent: bfloat16 [16384, 2048], P('dp'), may hold values from -6 to 6
- kv_cotangent: float32 [16384, 256], P('dp'), may hold values from -6 to 6
Outputs:
- output: bfloat16 [16384, 2048], P('dp')
- input_grad: bfloat16 [16384, 2048], P('dp')
- shared_kv: bfloat16 [16384, 256], P('dp')
- grad_norm1: float32 [2048], P(('dp', 'tensor'))
- grad_query: float32 [2048, 2048], P('dp', 'tensor')
- grad_shared_kv: float32 [2048, 256], P(('dp', 'tensor'))
- grad_output: float32 [2048, 2048], P('tensor', 'dp')
- grad_norm2: float32 [2048], P(('dp', 'tensor'))
- grad_gate: float32 [2048, 5632], P('dp', 'tensor')
- grad_up: float32 [2048, 5632], P('dp', 'tensor')
- grad_down: float32 [5632, 2048], P('tensor', 'dp')
Inputs may be any that keep to these rules, and one draw needn't show every extreme that they name: `doc_lengths`: each row holds the lengths of 4 documents packed in order into one sequence; a row sums to 1024, and its longest document has 512 tokens.
All inputs are finite; a program needn't handle non-finite values.
Results may differ from a plain program's by a relative error of at most 0.018.
Values may be sent and summed in bfloat16 or wider, within the bound.
A program may use at most 192 MiB of HBM per device.

v0:
```python
import math

import jax
import jax.numpy as jnp
from jax import lax
from jax.sharding import PartitionSpec as P

EPSILON = 1e-05
NEGATIVE = -1e30


def positions_of(doc_lengths, seq_len):
    ends = jnp.cumsum(doc_lengths, axis=1, dtype=jnp.int32)
    starts = ends - doc_lengths
    offsets = jnp.arange(seq_len, dtype=jnp.int32)
    segment = jnp.sum(
        (offsets[None, :, None] >= ends[:, None, :]).astype(jnp.int32), axis=2, dtype=jnp.int32
    )
    labels = jnp.arange(doc_lengths.shape[1], dtype=jnp.int32)
    chosen = segment[:, :, None] == labels[None, None, :]
    first_row = jnp.sum(jnp.where(chosen, starts[:, None, :], 0), axis=2, dtype=jnp.int32)
    return (segment, offsets[None, :] - first_row)


def rope_tables(position, head_dim):
    counter = jnp.arange(head_dim // 2, dtype=jnp.float32)
    inverse = jnp.exp(counter * (-2.0 * math.log(10000.0) / head_dim))
    angle = position.astype(jnp.float32)[..., None] * inverse
    return (jnp.cos(angle), jnp.sin(angle))


def rotate(values, cosine, sine):
    middle = values.shape[-1] // 2
    former = values[..., :middle]
    latter = values[..., middle:]
    return jnp.concatenate(
        [former * cosine - latter * sine, latter * cosine + former * sine], axis=-1
    )


def normalize(values):
    factor = lax.rsqrt(jnp.mean(values * values, axis=-1, keepdims=True) + EPSILON)
    return (values * factor, factor)


def norm_backward(d_normed, gain, normed, factor):
    scaled = d_normed * gain
    return factor * (scaled - normed * jnp.mean(scaled * normed, axis=-1, keepdims=True))


def allowed_of(segment_row):
    offsets = jnp.arange(segment_row.shape[0], dtype=jnp.int32)
    same_doc = segment_row[:, None] == segment_row[None, :]
    return same_doc & (offsets[:, None] >= offsets[None, :])


def masked_scores(query_seq, key_seq, segment_row):
    factor = 1.0 / math.sqrt(query_seq.shape[-1])
    scores = (
        jnp.einsum("qhd,kd->hqk", query_seq, key_seq, preferred_element_type=jnp.float32) * factor
    )
    return jnp.where(allowed_of(segment_row)[None], scores, NEGATIVE)


def attend_forward(operands):
    query_seq, key_seq, value_seq, segment_row = operands
    scores = masked_scores(query_seq, key_seq, segment_row)
    highest = jnp.max(scores, axis=-1, keepdims=True)
    log_total = highest + jnp.log(jnp.sum(jnp.exp(scores - highest), axis=-1, keepdims=True))
    weights = jnp.exp(scores - log_total).astype(jnp.bfloat16)
    attended = jnp.einsum("hqk,kd->qhd", weights, value_seq, preferred_element_type=jnp.float32)
    return (attended.astype(jnp.bfloat16), log_total)


def attend_backward(operands):
    query_seq, key_seq, value_seq, segment_row, log_total, d_attended = operands
    factor = 1.0 / math.sqrt(query_seq.shape[-1])
    weights = jnp.exp(masked_scores(query_seq, key_seq, segment_row) - log_total)
    d_weights = jnp.einsum("qhd,kd->hqk", d_attended, value_seq, preferred_element_type=jnp.float32)
    delta = jnp.sum(weights * d_weights, axis=-1, keepdims=True)
    d_scores = (weights * (d_weights - delta)).astype(jnp.bfloat16)
    d_query = (
        jnp.einsum("hqk,kd->qhd", d_scores, key_seq, preferred_element_type=jnp.float32) * factor
    )
    d_key = (
        jnp.einsum("hqk,qhd->kd", d_scores, query_seq, preferred_element_type=jnp.float32) * factor
    )
    d_value = jnp.einsum(
        "hqk,qhd->kd", weights.astype(jnp.bfloat16), d_attended, preferred_element_type=jnp.float32
    )
    return (d_query, d_key, d_value)


def tensor_total(values):
    return lax.psum(values, "tensor")


def per_device(
    inputs,
    doc_lengths,
    norm1_gain,
    w_query,
    w_shared_kv,
    w_output,
    norm2_gain,
    w_gate,
    w_up,
    w_down,
    out_cotangent,
    kv_cotangent,
):
    seq_count = doc_lengths.shape[0]
    token_count = inputs.shape[0]
    seq_len = token_count // seq_count
    head_dim = w_shared_kv.shape[1] // 2
    local_heads = w_query.shape[1] // head_dim
    segment, position = positions_of(doc_lengths, seq_len)
    cosine, sine = rope_tables(position, head_dim)
    head_cos = cosine[:, :, None, :]
    head_sin = sine[:, :, None, :]
    tensor_rank = lax.axis_index("tensor")
    leader = tensor_rank == 0
    inputs_wide = inputs.astype(jnp.float32)
    normed1, factor1 = normalize(inputs_wide)
    n1_low = (normed1 * norm1_gain).astype(jnp.bfloat16)
    query = jnp.dot(n1_low, w_query, preferred_element_type=jnp.float32)
    kv_pre = jnp.dot(n1_low, w_shared_kv, preferred_element_type=jnp.float32)
    query_rot = rotate(
        query.reshape(seq_count, seq_len, local_heads, head_dim), head_cos, head_sin
    ).astype(jnp.bfloat16)
    key_rot = rotate(
        kv_pre[:, :head_dim].reshape(seq_count, seq_len, head_dim), cosine, sine
    ).astype(jnp.bfloat16)
    value_low = kv_pre[:, head_dim:].astype(jnp.bfloat16).reshape(seq_count, seq_len, head_dim)
    shared_kv = jnp.concatenate([key_rot, value_low], axis=-1).reshape(token_count, 2 * head_dim)
    attended, log_total = lax.map(attend_forward, (query_rot, key_rot, value_low, segment))
    attended_flat = attended.reshape(token_count, local_heads * head_dim)
    branch_part = jnp.dot(attended_flat, w_output, preferred_element_type=jnp.float32)
    hidden1 = inputs_wide + tensor_total(branch_part)
    normed2, factor2 = normalize(hidden1)
    n2_low = (normed2 * norm2_gain).astype(jnp.bfloat16)
    gate_pre = jnp.dot(n2_low, w_gate, preferred_element_type=jnp.float32)
    up_pre = jnp.dot(n2_low, w_up, preferred_element_type=jnp.float32)
    sigmoid_gate = jax.nn.sigmoid(gate_pre)
    silu_gate = gate_pre * sigmoid_gate
    hidden = (silu_gate * up_pre).astype(jnp.bfloat16)
    mlp_part = jnp.dot(hidden, w_down, preferred_element_type=jnp.float32)
    output = (hidden1 + tensor_total(mlp_part)).astype(jnp.bfloat16)
    out_wide = out_cotangent.astype(jnp.float32)
    d_hidden = jnp.dot(out_cotangent, w_down.T, preferred_element_type=jnp.float32)
    grad_down = jnp.dot(hidden.T, out_cotangent, preferred_element_type=jnp.float32)
    d_gate = (d_hidden * up_pre * sigmoid_gate * (1.0 + gate_pre * (1.0 - sigmoid_gate))).astype(
        jnp.bfloat16
    )
    d_up = (d_hidden * silu_gate).astype(jnp.bfloat16)
    grad_gate = jnp.dot(n2_low.T, d_gate, preferred_element_type=jnp.float32)
    grad_up = jnp.dot(n2_low.T, d_up, preferred_element_type=jnp.float32)
    d_n2_part = jnp.dot(d_gate, w_gate.T, preferred_element_type=jnp.float32) + jnp.dot(
        d_up, w_up.T, preferred_element_type=jnp.float32
    )
    d_n2 = tensor_total(d_n2_part)
    grad_norm2 = jnp.where(leader, jnp.sum(d_n2 * normed2, axis=0), 0.0)
    d_h1 = out_wide + norm_backward(d_n2, norm2_gain, normed2, factor2)
    d_branch = d_h1.astype(jnp.bfloat16)
    grad_output = jnp.dot(attended_flat.T, d_branch, preferred_element_type=jnp.float32)
    d_attended = jnp.dot(d_branch, w_output.T, preferred_element_type=jnp.float32).astype(
        jnp.bfloat16
    )
    d_attended = d_attended.reshape(seq_count, seq_len, local_heads, head_dim)
    d_query_rot, d_key_rot, d_value = lax.map(
        attend_backward, (query_rot, key_rot, value_low, segment, log_total, d_attended)
    )
    kv_part = jnp.concatenate([d_key_rot, d_value], axis=-1).reshape(token_count, 2 * head_dim)
    d_kv_rot = lax.psum(kv_part, "tensor") + kv_cotangent
    d_kv_rot = d_kv_rot.reshape(seq_count, seq_len, 2 * head_dim)
    d_key = rotate(d_kv_rot[..., :head_dim], cosine, -sine)
    d_kv = (
        jnp.concatenate([d_key, d_kv_rot[..., head_dim:]], axis=-1)
        .astype(jnp.bfloat16)
        .reshape(token_count, 2 * head_dim)
    )
    d_query = (
        rotate(d_query_rot, head_cos, -head_sin)
        .astype(jnp.bfloat16)
        .reshape(token_count, local_heads * head_dim)
    )
    grad_query = jnp.dot(n1_low.T, d_query, preferred_element_type=jnp.float32)
    grad_kv = jnp.dot(n1_low.T, d_kv, preferred_element_type=jnp.float32)
    grad_query, grad_output, grad_gate, grad_up, grad_down = (
        lax.psum_scatter(
            grad_query.astype(jnp.bfloat16), "dp", scatter_dimension=0, tiled=True
        ).astype(jnp.float32),
        lax.psum_scatter(
            grad_output.astype(jnp.bfloat16), "dp", scatter_dimension=1, tiled=True
        ).astype(jnp.float32),
        lax.psum_scatter(
            grad_gate.astype(jnp.bfloat16), "dp", scatter_dimension=0, tiled=True
        ).astype(jnp.float32),
        lax.psum_scatter(
            grad_up.astype(jnp.bfloat16), "dp", scatter_dimension=0, tiled=True
        ).astype(jnp.float32),
        lax.psum_scatter(
            grad_down.astype(jnp.bfloat16), "dp", scatter_dimension=1, tiled=True
        ).astype(jnp.float32),
    )
    d_n1_part = jnp.dot(d_query, w_query.T, preferred_element_type=jnp.float32)
    d_n1 = tensor_total(d_n1_part) + jnp.dot(
        d_kv, w_shared_kv.T, preferred_element_type=jnp.float32
    )
    grad_norm1 = jnp.where(leader, jnp.sum(d_n1 * normed1, axis=0), 0.0)
    input_grad = (d_h1 + norm_backward(d_n1, norm1_gain, normed1, factor1)).astype(jnp.bfloat16)
    grad_kv = jnp.where(leader, grad_kv, 0.0)
    grad_kv, grad_norm1, grad_norm2 = (
        lax.psum_scatter(grad_kv, ("dp", "tensor"), scatter_dimension=0, tiled=True),
        lax.psum_scatter(grad_norm1, ("dp", "tensor"), scatter_dimension=0, tiled=True),
        lax.psum_scatter(grad_norm2, ("dp", "tensor"), scatter_dimension=0, tiled=True),
    )
    return (
        output,
        input_grad,
        shared_kv,
        grad_norm1,
        grad_query,
        grad_kv,
        grad_output,
        grad_norm2,
        grad_gate,
        grad_up,
        grad_down,
    )


def solution(mesh):
    placed = (
        P("dp", None),
        P("dp", None),
        P(),
        P(None, "tensor"),
        P(),
        P("tensor", None),
        P(),
        P(None, "tensor"),
        P(None, "tensor"),
        P("tensor", None),
        P("dp", None),
        P("dp", None),
    )
    return jax.shard_map(
        per_device,
        mesh=mesh,
        in_specs=placed,
        out_specs=(
            P("dp", None),
            P("dp", None),
            P("dp", None),
            P(("dp", "tensor")),
            P("dp", "tensor"),
            P(("dp", "tensor"), None),
            P("tensor", "dp"),
            P(("dp", "tensor")),
            P("dp", "tensor"),
            P("dp", "tensor"),
            P("tensor", "dp"),
        ),
        check_vma=False,
    )
```

profile of v0, /device:TPU:1, one launch (start us, length us, event | category | flops | bytes accessed | tf_op | source)
XLA Modules:
  0.0 1550.4 jit_solution(11970412418308403599)
XLA Ops:
  10.8 3.1 fusion.11
  16.5 3.4 fusion.52
  39.9 4.5 fusion.66
  45.0 106.5 %all-reduce.8.cloned.1.call-done = f32[1024,2048]{1,0:T(8,128)} async-done(((f32[1024,2048]{1,0:T(8,128)}), f32[1024,2048]{1,0:T(8,128)}) %all-reduce.8.cloned.1.call-update) | async-done | bytes 8388624 | tf_op jit(solution)/shard_map/psum | solution.py:95
  151.5 5.7 multiply_reduce_fusion.2
  160.6 6.7 fusion.68
  167.3 3.2 fusion.67
  170.5 5.4 multiply_convert_fusion.1
  175.9 3.5 fusion.70
  179.5 6.0 convolution_add_fusion.1
  185.6 7.4 fusion.69
  192.9 96.6 %all-reduce.10.cloned.1.call-done = f32[1024,2048]{1,0:T(8,128)} async-done(((f32[1024,2048]{1,0:T(8,128)}), f32[1024,2048]{1,0:T(8,128)}) %all-reduce.10.cloned.1.call-update) | async-done | bytes 8388624 | tf_op jit(solution)/shard_map/psum | solution.py:95
  289.6 7.6 multiply_reduce_fusion
  297.2 7.1 multiply_add_fusion
  307.6 3.4 convolution_bitcast_fusion
  313.9 2.9 fusion.14
  321.1 5.8 fusion.71
  328.1 5.8 convolution_convert_fusion.1
  336.7 6.0 convolution_convert_fusion
  346.0 5.9 convolution_convert_fusion.2
  354.8 5.0 convolution_convert_fusion.3
  361.2 4.7 convolution_convert_fusion.4
  366.4 154.9 %all-reduce.12.cloned.1.call-done = (f32[1024,2048]{1,0:T(8,128)}, f32[1024,2048]{1,0:T(8,128)}, f32[1024,256]{0,1:T(8,128)}) async-done(((f32[1024,2048]{1,0:T(8,128)}, f32[1024,2048]{1,0:T(8,128)}, f32[1024,256]{0,1:T(8,128)}), (f32[1024,2048]{1,0:T(8,128)}, f32[1024,2048]{1,0:T(8,128)}, f32[1024,256]{0,1:T(8,128)})) %all-reduce.12.cloned.1.call-update) | async-done | bytes 17825808 | tf_op jit(solution)/shard_map/psum | solution.py:95
  529.1 69.9 %reduce-scatter.21.cloned.1.call-done = bf16[128,704]{1,0:T(8,128)(2,1)} async-done(((bf16[2048,704]{1,0:T(8,128)(2,1)}), bf16[128,704]{1,0:T(8,128)(2,1)}) %reduce-scatter.21.cloned.1.call-update) | async-done | bytes 180240
  600.8 76.8 %reduce-scatter.23.cloned.1.call-done = bf16[128,704]{1,0:T(8,128)(2,1)} async-done(((bf16[2048,704]{1,0:T(8,128)(2,1)}), bf16[128,704]{1,0:T(8,128)(2,1)}) %reduce-scatter.23.cloned.1.call-update) | async-done | bytes 180240
  679.5 76.3 %reduce-scatter.25.cloned.1.call-done = bf16[128,704]{1,0:T(8,128)(2,1)} async-done(((bf16[2048,704]{1,0:T(8,128)(2,1)}), bf16[128,704]{1,0:T(8,128)(2,1)}) %reduce-scatter.25.cloned.1.call-update) | async-done | bytes 180240
  757.7 73.5 %reduce-scatter.19.cloned.1.call-done = bf16[128,256]{1,0:T(8,128)(2,1)} async-done(((bf16[2048,256]{1,0:T(8,128)(2,1)}), bf16[128,256]{1,0:T(8,128)(2,1)}) %reduce-scatter.19.cloned.1.call-update) | async-done | bytes 65552
  832.8 74.0 %reduce-scatter.15.cloned.1.call-done = bf16[128,256]{1,0:T(8,128)(2,1)} async-done(((bf16[2048,256]{1,0:T(8,128)(2,1)}), bf16[128,256]{1,0:T(8,128)(2,1)}) %reduce-scatter.15.cloned.1.call-update) | async-done | bytes 65552 | tf_op jit(solution)/shard_map/reduce_scatter | solution.py:190
  908.3 8.4 fusion.10
  916.8 67.1 %all-reduce.2 = (f32[2048]{0:T(1024)S(1)}, f32[2048]{0:T(1024)S(1)}) all-reduce(f32[2048]{0:T(1024)S(1)} %get-tuple-element.139, f32[2048]{0:T(1024)S(1)} %get-tuple-element.138), channel_id=2, replica_groups=mesh['dp'=16,'tensor'=8] {'dp','tensor'}, use_global_device_ids=true, to_apply=%region_16.17.clone | all-reduce | flops 4096 | bytes 32768
  985.0 18.3 %fusion.9 = (bf16[1024,2048]{1,0:T(8,128)(2,1)}, bf16[1024,2048]{1,0:T(8,128)(2,1)}) fusion(f32[1024,2048]{1,0:T(8,128)} %copy-done.3, bf16[1024,2048]{1,0:T(8,128)(2,1)} %param.12, f32[1024,2048]{1,0:T(8,128)} %get-tuple-element.137, f32[1024]{0:T(1024)S(1)} %broadcast_multiply_fusion, f32[2048]{0:T(1024)S(1)} %copy-done.34, f32[1024]{0:T(1024)S(1)} %copy-done.40, ...), kind=kLoop, calls=%fused_computation.12 | loop fusion | flops 20971520 | bytes 46153728 | tf_op jit(solution)/shard_map/convert_element_type | solution.py:211
  1003.3 540.4 %reduce-scatter.17.cloned.1.call-done = f32[16,256]{1,0:T(8,128)} async-done(((f32[2048,256]{1,0:T(8,128)}), f32[16,256]{1,0:T(8,128)}) %reduce-scatter.17.cloned.1.call-update) | async-done | bytes 16400 | tf_op jit(solution)/shard_map/reduce_scatter | solution.py:214
  (176 shorter events, 69.8 us)
Async XLA Ops:
  7.2 163.3 %copy-start = (bf16[704,2048]{1,0:T(8,128)(2,1)S(1)}, bf16[704,2048]{1,0:T(8,128)(2,1)}, u32[]{:S(2)}) copy-start(bf16[704,2048]{1,0:T(8,128)(2,1)} %param.21) | copy-start | bytes 8650756
  7.2 6.7 copy-start.33
  7.2 144.3 %all-reduce.8.cloned.1.call-start = ((), (), s32[]{:S(2)}) async-start(), calls=%async_computation.6 | async-start | bytes 16777216 | tf_op jit(solution)/shard_map/psum | solution.py:95
  7.3 12.7 copy-start.42
  10.8 9.1 copy-start.37
  15.2 6.5 copy-start.13
  15.2 6.5 copy-start.27
  16.5 6.5 copy-start.21
  44.4 112.9 %copy-start.32 = (f32[2048]{0:T(1024)S(1)}, f32[2048]{0:T(1024)}, u32[]{:S(2)}) copy-start(f32[2048]{0:T(1024)} %param.18) | copy-start | bytes 24580
  44.4 245.1 %all-reduce.10.cloned.1.call-start = ((), (), s32[]{:S(2)}) async-start(), calls=%async_computation.7 | async-start | bytes 16777216 | tf_op jit(solution)/shard_map/psum | solution.py:95
  160.6 6.7 copy-start.10
  160.6 6.7 copy-start.44
  185.5 335.7 %all-reduce.12.cloned.1.call-start = ((), (), s32[]{:S(2)}) async-start(), calls=%async_computation.14 | async-start | bytes 35651584 | tf_op jit(solution)/shard_map/psum | solution.py:95
  192.9 104.3 %copy-start.36 = (f32[1024]{0:T(1024)S(1)}, f32[1024]{0:T(1024)}, u32[]{:S(2)}) copy-start(f32[1024]{0:T(1024)} %copy-done.35) | copy-start | bytes 12292
  289.6 7.7 copy-start.9
  289.6 18.1 %slice-start = ((s8[8388608]{0:T(1024)(128)(4,1)}), s8[4194304]{0:T(1024)(128)(4,1)S(1)}, s32[]{:S(2)}) async-start(s8[8388608]{0:T(1024)(128)(4,1)} %bitcast.126), calls=%async_computation.15 | async-start | bytes 8388608
  297.2 7.2 copy-start.12
  297.2 10.4 slice-start.1
  321.1 5.8 copy-start.31
  328.0 271.0 %reduce-scatter.21.cloned.1.call-start = ((), (), s32[]{:S(2)}) async-start(), calls=%async_computation.11 | async-start | bytes 3342336
  336.7 341.0 %reduce-scatter.23.cloned.1.call-start = ((), (), s32[]{:S(2)}) async-start(), calls=%async_computation.12 | async-start | bytes 3342336
  345.6 410.3 %reduce-scatter.25.cloned.1.call-start = ((), (), s32[]{:S(2)}) async-start(), calls=%async_computation.13 | async-start | bytes 3342336
  354.8 476.4 %reduce-scatter.19.cloned.1.call-start = ((), (), s32[]{:S(2)}) async-start(), calls=%async_computation.10 | async-start | bytes 1114112
  361.2 545.6 %reduce-scatter.15.cloned.1.call-start = ((), (), s32[]{:S(2)}) async-start(), calls=%async_computation.8 | async-start | bytes 1114112 | tf_op jit(solution)/shard_map/reduce_scatter | solution.py:190
  365.9 156.9 %copy-start.38 = (f32[1024]{0:T(1024)S(1)}, f32[1024]{0:T(1024)}, u32[]{:S(2)}) copy-start(f32[1024]{0:T(1024)} %copy-done.37) | copy-start | bytes 12292
  365.9 156.9 %copy-start.43 = (f32[64]{0:T(128)S(1)}, f32[64]{0:T(128)}, u32[]{:S(2)}) copy-start(f32[64]{0:T(128)} %copy-done.42) | copy-start | bytes 772
  365.9 1177.8 %reduce-scatter.17.cloned.1.call-start = ((), (), s32[]{:S(2)}) async-start(), calls=%async_computation.9 | async-start | bytes 2113536 | tf_op jit(solution)/shard_map/reduce_scatter | solution.py:214
  526.8 381.5 %copy-start.29 = (bf16[2048,256]{1,0:T(8,128)(2,1)S(1)}, bf16[2048,256]{1,0:T(8,128)(2,1)}, u32[]{:S(2)}) copy-start(bf16[2048,256]{1,0:T(8,128)(2,1)} %param.16) | copy-start | bytes 3145732
  526.8 381.5 %copy-start.34 = (f32[2048]{0:T(1024)S(1)}, f32[2048]{0:T(1024)}, u32[]{:S(2)}) copy-start(f32[2048]{0:T(1024)} %param.14) | copy-start | bytes 24580
  526.8 381.5 %copy-start.40 = (f32[1024]{0:T(1024)S(1)}, f32[1024]{0:T(1024)}, u32[]{:S(2)}) copy-start(f32[1024]{0:T(1024)} %copy-done.39) | copy-start | bytes 12292
  908.3 8.4 copy-start.41
  985.0 558.7 %copy-start.1 = (bf16[704,2048]{1,0:T(8,128)(2,1)S(1)}, bf16[704,2048]{1,0:T(8,128)(2,1)}, u32[]{:S(2)}) copy-start(bf16[704,2048]{1,0:T(8,128)(2,1)} %param.21) | copy-start | bytes 8650756
  (27 other events, 78.4 us)
Sparse Core Ops, SparseCore 0:
  44.5 106.9 all-reduce.7
  185.6 103.8 all-reduce.9
  328.1 193.0 all-reduce.11
  524.5 74.4 reduce-scatter.20
  602.7 74.8 reduce-scatter.22
  680.9 74.9 reduce-scatter.24
  759.0 72.0 reduce-scatter.18
  834.7 72.0 reduce-scatter.14
  909.7 633.9 reduce-scatter.16
where the time goes:
time: 1560 us; the launch traced here: 1550 us
  waiting for transfers between devices  1270 us (81%)
  matrix products  99.3 us (6%)
  other arithmetic  68.3 us (4%)
  blocking collectives  67.1 us (4%)
  local copies, waits for them, and re-layouts  30.5 us (2%)
    reduce_scatter x1, waiting for transfers between devices, per_device(): lax.psum_scatter(grad_kv, ('dp', 'tensor'), scatter_dimension=0, tiled=True)  540 us
    psum x3, waiting for transfers between devices, tensor_total(): return lax.psum(values, 'tensor')  358 us
    unnamed x13, waiting for transfers between devices  297 us
    reduce_scatter x1, waiting for transfers between devices, per_device(): lax.psum_scatter(grad_query.astype(jnp.bfloat16), 'dp', scatter_dimension...  74 us
    unnamed x1, blocking collectives  67.1 us
  transfers between devices with their start and end apart: 9, of which 9 were waited for; matrix products, arithmetic and copies ran while one was open for 6% of the time, Pallas kernels for 0%

commit v1 on v0

v1 whole, which is shorter than its diff:
```python
import functools
import math

import jax
import jax.numpy as jnp
from jax import lax
from jax.experimental import pallas as pl
from jax.experimental.pallas import tpu as pltpu
from jax.sharding import PartitionSpec as P

EPSILON = 1e-05
NEGATIVE = -1e30
MESH = pl.DeviceIdType.MESH
F32, BF16 = jnp.float32, jnp.bfloat16
VM = pl.BlockSpec(memory_space=pltpu.VMEM)
ANY = pl.BlockSpec(memory_space=pl.ANY)


class Links:
    def __init__(self, send, recv):
        dp, t = lax.axis_index("dp"), lax.axis_index("tensor")
        self.dp, self.t = dp, t
        self.x, self.y, self.z, self.c = dp // 4, dp % 4, t // 2, t % 2
        self.send, self.recv, self.used = send, recv, 0
        self.sent = []

    def slot(self, d, c=None):
        return 2 * ((self.z + d) % 4) + (self.c if c is None else c)

    def zdev(self, d):
        return (self.dp, self.slot(d))

    def sib(self):
        return (self.dp, self.slot(0, 1 - self.c))

    def xdev(self, d):
        return (((self.x + d) % 4) * 4 + self.y, self.t)

    def ydev(self, d):
        return (self.x * 4 + (self.y + d) % 4, self.t)

    def barrier(self, devs):
        b = pltpu.get_barrier_semaphore()
        for dev in devs:
            pl.semaphore_signal(b, inc=1, device_id=dev, device_id_type=MESH)
        pl.semaphore_wait(b, len(devs))

    def cp(self, src, dst, dev):
        copy = pltpu.make_async_remote_copy(
            src_ref=src,
            dst_ref=dst,
            send_sem=self.send.at[self.used],
            recv_sem=self.recv.at[self.used],
            device_id=dev,
            device_id_type=MESH,
        )
        self.used += 1
        copy.start()
        self.sent.append(copy)
        return copy

    def drain(self):
        for copy in self.sent:
            copy.wait_send()
        self.sent = []


def slabs(rows, step, body):
    if rows == step:
        body(pl.ds(0, step))
        return

    def one(i, carry):
        body(pl.ds(pl.multiple_of(i * step, step), step))
        return carry

    lax.fori_loop(0, rows // step, one, 0)


def add_rows(dst, src, rows, step=32):
    def body(s):
        dst[s] = dst[s] + src[s]

    slabs(rows, step, body)


def rs_z(k, part, rc, acc, hp, hm, fp, fm):
    order = (2, 1, 3, 0)
    swap = [k.cp(part.at[k.slot(d, 1 - k.c)], rc.at[i], k.sib()) for i, d in enumerate(order)]

    def core_add(i):
        swap[i].wait_recv()
        mine = part.at[k.slot(order[i])]

        def body(s):
            acc[i, s] = mine[s] + rc[i, s]

        slabs(128, 32, body)

    lo, hi = pl.ds(0, 64), pl.ds(64, 64)
    core_add(0)
    h1 = k.cp(acc.at[0, lo], hp, k.zdev(1))
    h2 = k.cp(acc.at[0, hi], hm, k.zdev(-1))
    core_add(1)
    u1 = k.cp(acc.at[1, hi], fp.at[hi], k.zdev(1))
    core_add(2)
    u2 = k.cp(acc.at[2, lo], fm.at[lo], k.zdev(-1))
    h1.wait_recv()
    add_rows(acc.at[1, lo], hp, 64)
    w1 = k.cp(acc.at[1, lo], fp.at[lo], k.zdev(1))
    h2.wait_recv()
    add_rows(acc.at[2, hi], hm, 64)
    w2 = k.cp(acc.at[2, hi], fm.at[hi], k.zdev(-1))
    core_add(3)
    for copy in (u1, u2, w1, w2):
        copy.wait_recv()


def ag_z(k, dst):
    lo, hi = pl.ds(0, 64), pl.ds(64, 64)
    me, below, above, far = k.t, k.slot(-1), k.slot(1), k.slot(2)
    a1 = k.cp(dst.at[me, lo], dst.at[me, lo], k.zdev(1))
    b1 = k.cp(dst.at[me, hi], dst.at[me, hi], k.zdev(-1))
    a2 = k.cp(dst.at[me, hi], dst.at[me, hi], k.zdev(1))
    b2 = k.cp(dst.at[me, lo], dst.at[me, lo], k.zdev(-1))
    s0 = k.cp(dst.at[me], dst.at[me], k.sib())
    a1.wait_recv()
    f1 = k.cp(dst.at[below, lo], dst.at[below, lo], k.zdev(1))
    b1.wait_recv()
    f2 = k.cp(dst.at[above, hi], dst.at[above, hi], k.zdev(-1))
    a2.wait_recv()
    s1 = k.cp(dst.at[below], dst.at[below], k.sib())
    b2.wait_recv()
    s2 = k.cp(dst.at[above], dst.at[above], k.sib())
    f1.wait_recv()
    f2.wait_recv()
    s3 = k.cp(dst.at[far], dst.at[far], k.sib())
    for copy in (s0, s1, s2, s3):
        copy.wait_recv()


def z_scratch(width):
    return [
        pltpu.VMEM((4, 128, width), BF16),
        pltpu.VMEM((4, 128, width), BF16),
        pltpu.VMEM((64, width), BF16),
        pltpu.VMEM((64, width), BF16),
        pltpu.VMEM((128, width), BF16),
        pltpu.VMEM((128, width), BF16),
    ]


def sems(n):
    return [pltpu.SemaphoreType.DMA((n,)), pltpu.SemaphoreType.DMA((n,))]


def own_sum(acc, fp, fm, s):
    return acc[3, s].astype(F32) + fp[s].astype(F32) + fm[s].astype(F32)


def z_barrier(k):
    k.barrier([k.zdev(1), k.zdev(-1), k.sib()])


def unit(values):
    factor = lax.rsqrt(jnp.mean(values * values, axis=-1, keepdims=True) + EPSILON)
    return values * factor, factor


def h1_kernel(part, x, gain, h1_out, n2_out, rc, acc, hp, hm, fp, fm, send, recv):
    k = Links(send, recv)
    z_barrier(k)
    rs_z(k, part, rc, acc, hp, hm, fp, fm)

    def body(s):
        h1 = x[k.t, s].astype(F32) + own_sum(acc, fp, fm, s)
        h1_out[s] = h1
        n2_out[k.t, s] = (unit(h1)[0] * gain[...]).astype(BF16)

    slabs(128, 16, body)
    ag_z(k, n2_out)
    k.drain()


def out_kernel(part, h1, y_out, rc, acc, hp, hm, fp, fm, send, recv):
    k = Links(send, recv)
    z_barrier(k)
    rs_z(k, part, rc, acc, hp, hm, fp, fm)

    def body(s):
        y_out[k.t, s] = (h1[s] + own_sum(acc, fp, fm, s)).astype(BF16)

    slabs(128, 16, body)
    ag_z(k, y_out)
    k.drain()


def norm_back(d_normed, gain, normed, factor):
    scaled = d_normed * gain
    return factor * (scaled - normed * jnp.mean(scaled * normed, axis=-1, keepdims=True))


def dn2_kernel(part, oc, h1, gain, dh1_out, db_out, gnorm, rc, acc, hp, hm, fp, fm, send, recv):
    k = Links(send, recv)
    z_barrier(k)
    rs_z(k, part, rc, acc, hp, hm, fp, fm)
    gnorm[...] = jnp.zeros_like(gnorm)

    def body(s):
        d = own_sum(acc, fp, fm, s)
        y2, r2 = unit(h1[s])
        dh1 = oc[k.t, s].astype(F32) + norm_back(d, gain[...], y2, r2)
        dh1_out[s] = dh1
        db_out[k.t, s] = dh1.astype(BF16)
        dy = d * y2
        gnorm[...] += dy[0:8] + dy[8:16]

    slabs(128, 16, body)
    ag_z(k, db_out)
    k.drain()


def dot(a, b, dims=((1,), (0,))):
    return lax.dot_general(a, b, (dims, ((), ())), preferred_element_type=F32)


def rope_cols(values, cos, sin):
    return values * cos + pltpu.roll(values, 64, axis=1) * sin


def dn1_kernel(
    part, kvpart, kvct, cos, sin, wkv, x, dh1, gain, n1,
    ig_out, gkv_out, gnorm,
    rc, acc, hp, hm, fp, fm, kvrc, kvacc, kvin, dkv, send, recv,
):
    k = Links(send, recv)
    k.barrier([k.zdev(1), k.zdev(-1), k.zdev(2), k.sib()])
    swap = k.cp(kvpart.at[1 - k.c], kvrc, k.sib())
    rs_z(k, part, rc, acc, hp, hm, fp, fm)
    swap.wait_recv()
    kvacc[...] = kvpart[k.c] + kvrc[...]
    got = [
        k.cp(kvacc.at[(k.z + d) % 4], kvin.at[d - 1], k.zdev(d)) for d in (1, 2, 3)
    ]
    for copy in got:
        copy.wait_recv()
    total = kvacc[k.z].astype(F32) + kvct[k.t]
    for d in range(3):
        total = total + kvin[d].astype(F32)
    dkv[:, 0:128] = rope_cols(total[:, 0:128], cos[k.t], -sin[k.t]).astype(BF16)
    dkv[:, 128:256] = total[:, 128:256].astype(BF16)
    gkv_out[...] = dot(n1[k.t], dkv[...], ((0,), (0,))).astype(BF16)
    gnorm[...] = jnp.zeros_like(gnorm)

    def body(s):
        d = own_sum(acc, fp, fm, s) + dot(dkv[s], wkv[...], ((1,), (1,)))
        y1, r1 = unit(x[k.t, s].astype(F32))
        ig_out[k.t, s] = (dh1[s] + norm_back(d, gain[...], y1, r1)).astype(BF16)
        dy = d * y1
        gnorm[...] += dy[0:8] + dy[8:16]

    slabs(128, 16, body)
    ag_z(k, ig_out)
    k.drain()


def rs4(k, view, hp, hm, fp, fm, dev, halves, add, fin):
    h1 = k.cp(view(2, 0), hp, dev(1))
    h2 = k.cp(view(2, 1), hm, dev(-1))
    u1 = k.cp(view(1, 1), halves(fp, 1), dev(1))
    u2 = k.cp(view(3, 0), halves(fm, 0), dev(-1))
    yield
    h1.wait_recv()
    add(view(1, 0), hp)
    w1 = k.cp(view(1, 0), halves(fp, 0), dev(1))
    h2.wait_recv()
    add(view(3, 1), hm)
    w2 = k.cp(view(3, 1), halves(fm, 1), dev(-1))
    yield
    for copy in (u1, w1, u2, w2):
        copy.wait_recv()
    fin()


def add3(dst, a, b):
    dst[...] = (dst[...].astype(F32) + a[...].astype(F32) + b[...].astype(F32)).astype(dst.dtype)


def gr_kernel(
    g_in, kv_in, g_out, kv_out,
    g, hp1, hm1, fp1, fm1, hp2, hm2, fp2, fm2, kvrc, kvacc, kvz, kvx, kvy, copy_sem, send, recv,
):
    R = g.shape[2]
    H, Q = R // 2, R // 4
    k = Links(send, recv)
    load = pltpu.make_async_copy(g_in, g, copy_sem)
    load.start()
    k.barrier(
        [k.sib()] + [dev(d) for dev in (k.xdev, k.ydev, k.zdev) for d in (1, 2, 3)]
    )
    swap = k.cp(kv_in.at[:, pl.ds(4 * (1 - k.c), 4)], kvrc, k.sib())
    load.wait()

    def wide_half(f, h):
        return f.at[pl.ds(2 * h, 2)]

    def wide_add(dst, src):
        for i in range(2):
            slabs(H, Q, lambda s: dst.__setitem__((i, s), dst[i, s] + src[i, s]))

    def thin_half(f, h):
        return f.at[0, pl.ds(Q * h, Q)]

    def thin_add(dst, src):
        slabs(Q, Q, lambda s: dst.__setitem__(s, dst[s] + src[s]))

    def wide_fin(own, fp, fm):
        def fin():
            for i in range(4):
                def body(s):
                    own(i)[s] = (own(i)[s].astype(F32) + fp[i, s].astype(F32) + fm[i, s].astype(F32)).astype(BF16)
                slabs(H, Q, body)
        return fin

    def thin_fin(own, fp, fm, at):
        def fin():
            def body(s):
                g_out[pl.ds(at + s.start, s.size)] = (
                    own[s].astype(F32) + fp[0, s].astype(F32) + fm[0, s].astype(F32)
                )
            slabs(H, Q, body)
        return fin

    first = pl.ds(0, H)
    second = pl.ds(H, H)
    a1 = rs4(
        k, lambda d, h: g.at[(k.x + d) % 4, pl.ds(2 * h, 2), first],
        hp1, hm1, fp1, fm1, k.xdev, wide_half, wide_add,
        wide_fin(lambda i: g.at[k.x, i, first], fp1, fm1),
    )
    b1 = rs4(
        k, lambda d, h: g.at[pl.ds(2 * h, 2), (k.y + d) % 4, second],
        hp2, hm2, fp2, fm2, k.ydev, wide_half, wide_add,
        wide_fin(lambda i: g.at[i, k.y, second], fp2, fm2),
    )
    next(a1); next(b1)
    swap.wait_recv()
    for i in range(16):
        kvacc[i] = kv_in[i, pl.ds(4 * k.c, 4)] + kvrc[i]
    next(a1); next(b1)
    zin = [k.cp(kvacc.at[:, (k.z + d) % 4], kvz.at[d - 1], k.zdev(d)) for d in (1, 2, 3)]
    for copy in zin:
        copy.wait_recv()
    kvz[3] = kvacc[:, k.z]
    kvz[3] = (sum(kvz[i].astype(F32) for i in range(4))).astype(BF16)
    for p in (a1, b1):
        for _ in p:
            pass
    xin = [k.cp(kvz.at[3, pl.ds(4 * ((k.x + d) % 4), 4)], kvx.at[d - 1], k.xdev(d)) for d in (1, 2, 3)]
    return k, xin


def body_gr(*refs):
    (g_in, kv_in, g_out, kv_out, g, hp1, hm1, fp1, fm1, hp2, hm2, fp2, fm2,
     kvrc, kvacc, kvz, kvx, kvy, tp1, tm1, tq1, tr1, tp2, tm2, tq2, tr2, copy_sem, send, recv) = refs
    k, xin = gr_kernel(
        g_in, kv_in, g_out, kv_out, g, hp1, hm1, fp1, fm1, hp2, hm2, fp2, fm2,
        kvrc, kvacc, kvz, kvx, kvy, copy_sem, send, recv)
    R = g.shape[2]
    H, Q = R // 2, R // 4

    def thin_half(f, h):
        return f.at[pl.ds(Q * h, Q)]

    def thin_add(dst, src):
        slabs(Q, Q, lambda s: dst.__setitem__(s, dst[s] + src[s]))

    def thin_fin(own, fp, fm, at):
        def fin():
            def body(i, carry):
                s = pl.ds(pl.multiple_of(i * Q, Q), Q)
                o = pl.ds(pl.multiple_of(at + i * Q, 8), Q)
                g_out[o] = own[s].astype(F32) + fp[s].astype(F32) + fm[s].astype(F32)
                return carry
            lax.fori_loop(0, 2, body, 0)
        return fin

    a2 = rs4(
        k, lambda d, h: g.at[k.x, (k.y + d) % 4, pl.ds(Q * h, Q)],
        tp1, tm1, tq1, tr1, k.ydev, thin_half, thin_add,
        thin_fin(g.at[k.x, k.y, pl.ds(0, H)], tq1, tr1, 0),
    )
    b2 = rs4(
        k, lambda d, h: g.at[(k.x + d) % 4, k.y, pl.ds(H + Q * h, Q)],
        tp2, tm2, tq2, tr2, k.xdev, thin_half, thin_add,
        thin_fin(g.at[k.x, k.y, pl.ds(H, H)], tq2, tr2, H),
    )
    next(a2); next(b2)
    for copy in xin:
        copy.wait_recv()
    kvx[3] = (kvz[3, pl.ds(4 * k.x, 4)].astype(F32) + sum(kvx[i].astype(F32) for i in range(3))).astype(BF16)
    yin = [k.cp(kvx.at[3, (k.y + d) % 4], kvy.at[d - 1], k.ydev(d)) for d in (1, 2, 3)]
    next(a2); next(b2)
    for copy in yin:
        copy.wait_recv()
    kv_out[...] = kvx[3, k.y].astype(F32) + sum(kvy[i].astype(F32) for i in range(3))
    for p in (a2, b2):
        for _ in p:
            pass
    k.drain()


def call(kernel, cid, outs, ins, scratch, in_specs=None, limit=60):
    return pl.pallas_call(
        kernel,
        out_shape=[jax.ShapeDtypeStruct(s, d) for s, d in outs],
        in_specs=in_specs or [VM] * len(ins),
        out_specs=[VM] * len(outs),
        scratch_shapes=scratch,
        compiler_params=pltpu.CompilerParams(
            collective_id=cid, has_side_effects=True, vmem_limit_bytes=limit * 2**20
        ),
    )(*ins)


def positions_of(doc_lengths, seq_len):
    ends = jnp.cumsum(doc_lengths, axis=1, dtype=jnp.int32)
    starts = ends - doc_lengths
    offsets = jnp.arange(seq_len, dtype=jnp.int32)
    segment = jnp.sum(
        (offsets[None, :, None] >= ends[:, None, :]).astype(jnp.int32), axis=2, dtype=jnp.int32
    )
    labels = jnp.arange(doc_lengths.shape[1], dtype=jnp.int32)
    chosen = segment[:, :, None] == labels[None, None, :]
    first_row = jnp.sum(jnp.where(chosen, starts[:, None, :], 0), axis=2, dtype=jnp.int32)
    return (segment, offsets[None, :] - first_row)


def rope_tables(position, head_dim):
    counter = jnp.arange(head_dim // 2, dtype=jnp.float32)
    inverse = jnp.exp(counter * (-2.0 * math.log(10000.0) / head_dim))
    angle = position.astype(jnp.float32)[..., None] * inverse
    return (jnp.cos(angle), jnp.sin(angle))


def rotate(values, cosine, sine):
    middle = values.shape[-1] // 2
    former = values[..., :middle]
    latter = values[..., middle:]
    return jnp.concatenate(
        [former * cosine - latter * sine, latter * cosine + former * sine], axis=-1
    )


def masked_scores(query_seq, key_seq, segment_row):
    offsets = jnp.arange(segment_row.shape[0], dtype=jnp.int32)
    allowed = (segment_row[:, None] == segment_row[None, :]) & (offsets[:, None] >= offsets[None, :])
    factor = 1.0 / math.sqrt(query_seq.shape[-1])
    scores = jnp.einsum("qhd,kd->hqk", query_seq, key_seq, preferred_element_type=F32) * factor
    return jnp.where(allowed[None], scores, NEGATIVE)


def per_device(
    inputs, doc_lengths, norm1_gain, w_query, w_shared_kv, w_output, norm2_gain,
    w_gate, w_up, w_down, out_cotangent, kv_cotangent,
):
    segment, position = positions_of(doc_lengths, 1024)
    segment = segment[0]
    cosine, sine = rope_tables(position[0], 128)
    head_cos, head_sin = cosine[:, None, :], sine[:, None, :]
    x = inputs.astype(F32)
    y1, r1 = unit(x)
    n1 = (y1 * norm1_gain).astype(BF16)
    query = jnp.dot(n1, w_query, preferred_element_type=F32)
    kv_pre = jnp.dot(n1, w_shared_kv, preferred_element_type=F32)
    query_rot = rotate(query.reshape(1024, 2, 128), head_cos, head_sin).astype(BF16)
    key_rot = rotate(kv_pre[:, :128], cosine, sine).astype(BF16)
    value = kv_pre[:, 128:].astype(BF16)
    shared_kv = jnp.concatenate([key_rot, value], axis=-1)
    scores = masked_scores(query_rot, key_rot, segment)
    highest = jnp.max(scores, axis=-1, keepdims=True)
    grown = jnp.exp(scores - highest)
    probs = grown / jnp.sum(grown, axis=-1, keepdims=True)
    probs_low = probs.astype(BF16)
    attended = jnp.einsum("hqk,kd->qhd", probs_low, value, preferred_element_type=F32)
    attended = attended.astype(BF16).reshape(1024, 256)
    part = jnp.dot(attended, w_output, preferred_element_type=F32).astype(BF16)
    gain1, gain2 = norm1_gain.reshape(1, 2048), norm2_gain.reshape(1, 2048)
    cut = lambda v: v.reshape(8, 128, v.shape[-1])
    wide = ((8, 128, 2048), BF16)
    shard = ((128, 2048), F32)
    h1, n2 = call(h1_kernel, 0, [shard, wide], [cut(part), cut(inputs), gain2], z_scratch(2048) + sems(24))
    n2 = n2.reshape(1024, 2048)
    gate = jnp.dot(n2, w_gate, preferred_element_type=F32)
    up = jnp.dot(n2, w_up, preferred_element_type=F32)
    sig = jax.nn.sigmoid(gate)
    silu = gate * sig
    hidden = (silu * up).astype(BF16)
    part = jnp.dot(hidden, w_down, preferred_element_type=F32).astype(BF16)
    (output,) = call(out_kernel, 1, [wide], [cut(part), h1], z_scratch(2048) + sems(24))
    d_hidden = jnp.dot(out_cotangent, w_down.T, preferred_element_type=F32)
    g_down = jnp.dot(hidden.T, out_cotangent, preferred_element_type=F32).astype(BF16)
    d_gate = (d_hidden * up * sig * (1.0 + gate * (1.0 - sig))).astype(BF16)
    d_up = (d_hidden * silu).astype(BF16)
    g_gate = jnp.dot(d_gate.T, n2, preferred_element_type=F32).astype(BF16)
    g_up = jnp.dot(d_up.T, n2, preferred_element_type=F32).astype(BF16)
    part = (
        jnp.dot(d_gate, w_gate.T, preferred_element_type=F32)
        + jnp.dot(d_up, w_up.T, preferred_element_type=F32)
    ).astype(BF16)
    dh1, db, gn2 = call(
        dn2_kernel, 2, [shard, wide, ((8, 2048), F32)],
        [cut(part), cut(out_cotangent), h1, gain2], z_scratch(2048) + sems(24),
    )
    db = db.reshape(1024, 2048)
    g_out = jnp.dot(attended.T, db, preferred_element_type=F32).astype(BF16)
    d_att = jnp.dot(db, w_output.T, preferred_element_type=F32).astype(BF16).reshape(1024, 2, 128)
    d_probs = jnp.einsum("qhd,kd->hqk", d_att, value, preferred_element_type=F32)
    delta = jnp.sum(probs * d_probs, axis=-1, keepdims=True)
    d_scores = (probs * (d_probs - delta)).astype(BF16)
    factor = 1.0 / math.sqrt(128)
    d_query = jnp.einsum("hqk,kd->qhd", d_scores, key_rot, preferred_element_type=F32) * factor
    d_key = jnp.einsum("hqk,qhd->kd", d_scores, query_rot, preferred_element_type=F32) * factor
    d_value = jnp.einsum("hqk,qhd->kd", probs_low, d_att, preferred_element_type=F32)
    kvpart = jnp.concatenate([d_key, d_value], axis=-1).astype(BF16)
    kvpart = kvpart.reshape(4, 2, 128, 256).transpose(1, 0, 2, 3)
    d_query = rotate(d_query, head_cos, -head_sin).astype(BF16).reshape(1024, 256)
    g_query = jnp.dot(d_query.T, n1, preferred_element_type=F32).astype(BF16)
    part = jnp.dot(d_query, w_query.T, preferred_element_type=F32).astype(BF16)
    cos2 = jnp.concatenate([cosine, cosine], axis=-1)
    sin2 = jnp.concatenate([-sine, sine], axis=-1)
    kv4 = pltpu.VMEM((4, 128, 256), BF16)
    input_grad, gkv, gn1 = call(
        dn1_kernel, 3, [wide, ((2048, 256), BF16), ((8, 2048), F32)],
        [cut(part), kvpart, cut(kv_cotangent), cut(cos2), cut(sin2), w_shared_kv, cut(inputs), dh1, gain1, cut(n1)],
        z_scratch(2048) + [kv4, kv4, pltpu.VMEM((3, 128, 256), BF16), pltpu.VMEM((128, 256), BF16)] + sems(32),
    )
    gn = [jnp.broadcast_to(jnp.sum(v, axis=0)[:, None], (2048, 64)).astype(BF16) for v in (gn1, gn2)]
    kvall = jnp.concatenate([gkv] + gn, axis=-1).reshape(16, 8, 16, 384)
    kvall = kvall.reshape(16, 4, 2, 16, 384).transpose(0, 2, 1, 3, 4).reshape(16, 8, 16, 384)
    pieces = lambda v: v.reshape(v.shape[0], 16, 128).transpose(1, 0, 2)
    g = jnp.concatenate([pieces(v) for v in (g_down, g_gate, g_up, g_out, g_query)], axis=1)
    R = 2624
    H, Q = R // 2, R // 4
    b = lambda *s: pltpu.VMEM(s, BF16)
    gsum, kvsum = call(
        body_gr, 4, [((R, 128), F32), ((16, 384), F32)], [g.reshape(4, 4, R, 128), kvall],
        [b(4, 4, R, 128)]
        + [b(2, H, 128), b(2, H, 128), b(4, H, 128), b(4, H, 128)] * 2
        + [b(16, 4, 16, 384), b(16, 4, 16, 384), b(4, 16, 16, 384), b(4, 4, 16, 384), b(3, 16, 384)]
        + [b(Q, 128), b(Q, 128), b(H, 128), b(H, 128)] * 2
        + [pltpu.SemaphoreType.DMA] + sems(48),
        in_specs=[ANY, VM],
    )
    return (
        output.reshape(1024, 2048),
        input_grad.reshape(1024, 2048),
        shared_kv,
        kvsum[:, 256],
        gsum[2368:2624].T,
        kvsum[:, 0:256],
        gsum[2112:2368],
        kvsum[:, 320],
        gsum[704:1408].T,
        gsum[1408:2112].T,
        gsum[0:704],
    )


def solution(mesh):
    placed = (
        P("dp", None), P("dp", None), P(), P(None, "tensor"), P(), P("tensor", None), P(),
        P(None, "tensor"), P(None, "tensor"), P("tensor", None), P("dp", None), P("dp", None),
    )
    return jax.shard_map(
        per_device,
        mesh=mesh,
        in_specs=placed,
        out_specs=(
            P("dp", None), P("dp", None), P("dp", None), P(("dp", "tensor")), P("dp", "tensor"),
            P(("dp", "tensor"), None), P("tensor", "dp"), P(("dp", "tensor")), P("dp", "tensor"),
            P("dp", "tensor"), P("tensor", "dp"),
        ),
        check_vma=False,
    )
```

time: 1560 us -> 456 us (0.29)
  waiting for transfers between devices: 1270 us -> 0 us
  Pallas kernels: 0 us -> 289 us
  blocking collectives: 67.1 us -> 0 us
  other arithmetic: 68.3 us -> 32.9 us
  matrix products: 99.3 us -> 79 us
  local copies, waits for them, and re-layouts: 30.5 us -> 49.3 us
    reduce_scatter x2 -> x0, waiting for transfers between devices: 614 us -> none  [the longest x1 540 us: per_device(): lax.psum_scatter(grad_kv, ('dp', 'tensor'), scatter_dimension=0, tiled=True)]
    psum x3 -> x0, waiting for transfers between devices: 358 us -> none  [tensor_total(): return lax.psum(values, 'tensor')]
    unnamed x13 -> x0, waiting for transfers between devices: 297 us -> none
    pallas_call x0 -> x5, Pallas kernels: none -> 289 us  [call(): pl.pallas_call(kernel, out_shape=[jax.ShapeDtypeStruct(s, d) for s, d in...]
    unnamed x1 -> x0, blocking collectives: 67.1 us -> none
    dot_general x24 -> x22, matrix products: 99.3 us -> 79 us  [the longest x1 6.47 us: per_device(): gate = jnp.dot(n2, w_gate, preferred_element_type=F32)]
    convert_element_type x9 -> x3, other arithmetic: 27.4 us -> 7.33 us  [the longest x1 3.52 us: per_device(): probs_low = probs.astype(BF16)]
  transfers between devices with their start and end apart: 9 -> 0, of which waited for: 9 -> 0; matrix products, arithmetic and copies ran while one was open for 6% -> 0% of each run, Pallas kernels for 0% -> 0%
where the time goes in v1:
time: 456 us; the launch traced here: 452 us
  Pallas kernels  289 us (63%)
  matrix products  79 us (17%)
  local copies, waits for them, and re-layouts  49.3 us (11%)
  other arithmetic  32.9 us (7%)
    pallas_call x5, Pallas kernels, call(): pl.pallas_call(kernel, out_shape=[jax.ShapeDtypeStruct(s, d) for s, d in...  289 us
    unnamed x84, local copies, waits for them, and re-layouts  26.2 us

profile of v1, /device:TPU:1, one launch (start us, length us, event | category | flops | bytes accessed | tf_op | source)
XLA Modules:
  0.0 451.8 jit_solution(6576110493904553681)
XLA Ops:
  0.7 3.2 fusion
  10.0 3.0 fusion.33
  16.3 3.8 fusion.56
  21.1 2.4 copy.106
  25.9 2.9 subtract_convert_fusion.1
  28.8 3.1 fusion.15
  31.9 3.7 copy.69
  35.6 3.9 fusion.9
  41.6 3.5 fusion.5
  45.1 3.0 fusion.26
  48.9 3.3 convolution_convert_fusion.2
  52.2 54.5 %shard_map.203 = (f32[128,2048]{1,0:T(8,128)}, bf16[8,128,2048]{2,1,0:T(8,128)(2,1)}) custom-call(bf16[8,128,2048]{2,1,0:T(8,128)(2,1)} %bitcast.197, bf16[8,128,2048]{2,1,0:T(8,128)(2,1)} %bitcast.194, f32[1,2048]{1,0:T(1,128)} %bitcast.215), custom_call_target="tpu_custom_call" | custom-call | tf_op jit(solution)/shard_map/pallas_call | solution.py:414
  106.7 6.5 %fusion.57 = f32[1024,704]{0,1:T(8,128)S(1)} fusion(bf16[1024,2048]{1,0:T(8,128)(2,1)} %bitcast.218, bf16[2048,704]{0,1:T(8,128)(2,1)} %param.19), kind=kOutput, calls=%fused_computation.117 | convolution fusion | flops 2952790016 | bytes 9961472 | tf_op jit(solution)/shard_map/dot_general | solution.py:494
  113.3 3.2 fusion.58
  116.5 5.4 %multiply_convert_fusion = (bf16[1024,704]{0,1:T(8,128)(2,1)S(1)}, bf16[1024,704]{0,1:T(8,128)(2,1)S(1)}, bf16[1024,704]{0,1:T(8,128)(2,1)}) fusion(f32[1024,704]{0,1:T(8,128)S(1)} %fusion.57, f32[1024,704]{0,1:T(8,128)S(1)} %fusion.58, bf16[1024,2048]{1,0:T(8,128)(2,1)S(1)} %copy-done.9, bf16[704,2048]{1,0:T(8,128)(2,1)S(1)} %copy-done), kind=kOutput, calls=%fused_computation.38 | convolution fusion | flops 2963603456 | bytes 17170432 | tf_op jit(solution)/shard_map/dot_general | solution.py:501
  121.9 3.5 fusion.59
  125.4 5.3 %add_convert_fusion = bf16[1024,2048]{1,0:T(8,128)(2,1)} fusion(f32[1024,2048]{1,0:T(8,128)S(1)} %fusion.59, bf16[1024,704]{0,1:T(8,128)(2,1)S(1)} %get-tuple-element.66, bf16[2048,704]{0,1:T(8,128)(2,1)S(1)} %copy-done.28), kind=kOutput, calls=%fused_computation.15 | convolution fusion | flops 2956984320 | bytes 16908288 | tf_op jit(solution)/shard_map/dot_general | solution.py:509
  130.8 51.0 %shard_map.205 = (f32[128,2048]{1,0:T(8,128)}, bf16[8,128,2048]{2,1,0:T(8,128)(2,1)}, f32[8,2048]{1,0:T(8,128)}) custom-call(bf16[8,128,2048]{2,1,0:T(8,128)(2,1)} %bitcast.205, bf16[8,128,2048]{2,1,0:T(8,128)(2,1)} %bitcast.204, f32[128,2048]{1,0:T(8,128)} %get-tuple-element.22.h1, f32[1,2048]{1,0:T(1,128)} %bitcast.216), custom_call_target="tpu_custom_call" | custom-call | tf_op jit(solution)/shard_map/pallas_call | solution.py:414
  181.8 3.9 convolution_convert_fusion.8
  187.0 5.8 %fusion.6 = (f32[2,1024]{1,0:T(2,128)S(1)}, f32[1024,1024,2]{1,0,2:T(8,128)S(1)}) fusion(f32[2,1024]{1,0:T(2,128)S(1)} %fusion.11, f32[2,1024]{1,0:T(2,128)S(1)} %get-tuple-element.92, f32[1024,1024,2]{1,0,2:T(8,128)} %copy-done.1, pred[1024,1024]{0,1:T(8,128)(4,1)S(1)} %copy-done.5, bf16[1024,2,128]{0,2,1:T(8,128)(2,1)S(1)} %bitcast.225, ...), kind=kOutput, calls=%fused_computation.11 | convolution fusion | flops 549451776 | bytes 18636800 | tf_op jit(solution)/shard_map/qhd,kd->hqk/dot_general | solution.py:518
  192.9 2.8 fusion.8
  198.0 2.8 fusion.25
  207.1 4.6 %convolution_convert_fusion = bf16[1024,2048]{1,0:T(8,128)(2,1)} fusion(bf16[1024,256]{0,1:T(8,128)(2,1)S(1)} %bitcast.207, bf16[2048,256]{1,0:T(8,128)(2,1)} %param.15), kind=kOutput, calls=%fused_computation.26 | convolution fusion | flops 1075838976 | bytes 5767168 | tf_op jit(solution)/shard_map/dot_general | solution.py:529
  214.9 63.5 %shard_map.206 = (bf16[8,128,2048]{2,1,0:T(8,128)(2,1)}, bf16[2048,256]{1,0:T(8,128)(2,1)}, f32[8,2048]{1,0:T(8,128)}) custom-call(bf16[8,128,2048]{2,1,0:T(8,128)(2,1)} %bitcast.196, bf16[2,4,128,256]{3,2,1,0:T(8,128)(2,1)} %maximum_bitcast_fusion.kvpart, f32[8,128,256]{2,1,0:T(8,128)} %bitcast.212, f32[8,128,128]{2,1,0:T(8,128)} %get-tuple-element.96.cos, ...), custom_call_target="tpu_custom_call" | custom-call | tf_op jit(solution)/shard_map/pallas_call | solution.py:414
  284.9 3.4 fusion.21
  288.3 3.6 fusion.20
  291.9 2.4 fusion.18
  296.7 3.4 fusion.22
  308.6 70.8 %shard_map.207 = (f32[2624,128]{1,0:T(8,128)}, f32[16,384]{1,0:T(8,128)}) custom-call(bf16[4,4,2624,128]{3,2,1,0:T(8,128)(2,1)} %bitcast.43.refs_0_, bf16[16,8,16,384]{3,2,1,0:T(8,128)(2,1)} %bitcast.200), custom_call_target="tpu_custom_call" | custom-call | tf_op jit(solution)/shard_map/pallas_call | solution.py:414
  386.9 6.4 %convolution_convert_fusion.1 = bf16[1024,2048]{1,0:T(8,128)(2,1)} fusion(bf16[1024,704]{0,1:T(8,128)(2,1)} %get-tuple-element.68, bf16[704,2048]{1,0:T(8,128)(2,1)S(1)} %copy-done), kind=kOutput, calls=%fused_computation.27 | convolution fusion | flops 2954887168 | bytes 8519680 | tf_op jit(solution)/shard_map/dot_general | solution.py:499
  393.2 49.2 %shard_map.204 = bf16[8,128,2048]{2,1,0:T(8,128)(2,1)} custom-call(bf16[8,128,2048]{2,1,0:T(8,128)(2,1)} %bitcast.203, f32[128,2048]{1,0:T(8,128)} %get-tuple-element.22.h1), custom_call_target="tpu_custom_call" | custom-call | tf_op jit(solution)/shard_map/pallas_call | solution.py:414
  444.6 4.9 %copy.130 = bf16[1024,2048]{1,0:T(8,128)(2,1)} copy(bf16[1024,2048]{1,0:T(8,128)(2,1)} %bitcast.198) | data formatting | bytes 8388608
  (120 shorter events, 57.6 us)
Async XLA Ops:
  0.6 115.8 %copy-start = (bf16[704,2048]{1,0:T(8,128)(2,1)S(1)}, bf16[704,2048]{1,0:T(8,128)(2,1)}, u32[]{:S(2)}) copy-start(bf16[704,2048]{1,0:T(8,128)(2,1)} %param.21) | copy-start | bytes 8650756
  0.7 3.6 copy-start.2
  0.7 3.6 copy-start.23
  4.3 3.1 copy-start.18
  7.3 2.3 copy-start.29
  14.2 11.7 %copy-start.6 = (f32[1024,64]{1,0:T(8,128)}, f32[1024,64]{1,0:T(8,128)S(1)}, u32[]{:S(2)}) copy-start(f32[1024,64]{1,0:T(8,128)S(1)} %copy.71) | copy-start | bytes 786436
  35.6 3.9 copy-start.5
  39.5 5.6 %copy-start.1 = (f32[1024,1024,2]{1,0,2:T(8,128)}, f32[1024,1024,2]{1,0,2:T(8,128)S(1)}, u32[]{:S(2)}) copy-start(f32[1024,1024,2]{1,0,2:T(8,128)S(1)} %get-tuple-element.93) | copy-start | bytes 25165828
  41.6 3.5 copy-start.19
  45.1 3.8 copy-start.17
  106.7 6.5 %copy-start.24 = (bf16[8,128,2048]{2,1,0:T(8,128)(2,1)S(1)}, bf16[8,128,2048]{2,1,0:T(8,128)(2,1)}, u32[]{:S(2)}) copy-start(bf16[8,128,2048]{2,1,0:T(8,128)(2,1)} %get-tuple-element.21) | copy-start | bytes 12582916
  106.7 6.5 %copy-start.28 = (bf16[2048,704]{0,1:T(8,128)(2,1)S(1)}, bf16[2048,704]{0,1:T(8,128)(2,1)}, u32[]{:S(2)}) copy-start(bf16[2048,704]{0,1:T(8,128)(2,1)} %param.20) | copy-start | bytes 8650756
  113.3 3.2 copy-start.9
  116.5 5.4 %copy-start.27 = (bf16[2048,704]{0,1:T(8,128)(2,1)S(1)}, bf16[2048,704]{0,1:T(8,128)(2,1)}, u32[]{:S(2)}) copy-start(bf16[2048,704]{0,1:T(8,128)(2,1)} %param.19) | copy-start | bytes 8650756
  121.9 3.6 copy-start.30
  121.9 3.6 copy-start.32
  181.8 3.9 copy-start.11
  187.0 5.9 %slice-start = ((s8[8388608]{0:T(1024)(128)(4,1)}), s8[4194304]{0:T(1024)(128)(4,1)S(1)}, s32[]{:S(2)}) async-start(s8[8388608]{0:T(1024)(128)(4,1)} %bitcast.192), calls=%async_computation | async-start | bytes 8388608
  187.0 5.9 %slice-start.1 = ((s8[8388608]{0:T(1024)(128)(4,1)}), s8[4194304]{0:T(1024)(128)(4,1)S(1)}, s32[]{:S(2)}) async-start(s8[8388608]{0:T(1024)(128)(4,1)} %bitcast.192), calls=%async_computation.1 | async-start | bytes 8388608
  192.9 2.8 copy-start.21
  192.9 2.8 copy-start.22
  197.1 5.6 %copy-start.7 = (f32[1024,64]{1,0:T(8,128)S(1)}, f32[1024,64]{1,0:T(8,128)}, u32[]{:S(2)}) copy-start(f32[1024,64]{1,0:T(8,128)} %copy-done.6) | copy-start | bytes 786436
  281.3 3.6 copy-start.25
  281.3 3.6 copy-start.31
  284.9 3.4 copy-start.10
  284.9 3.4 copy-start.34
  294.3 2.4 copy-start.33
  300.0 2.4 copy-start.16
  300.1 3.4 copy-start.26
  303.4 2.6 copy-start.4
  393.2 50.3 %copy-start.14 = (bf16[1024,64]{0,1:T(8,128)(2,1)S(1)}, bf16[1024,64]{0,1:T(8,128)(2,1)}, u32[]{:S(2)}) copy-start(bf16[1024,64]{0,1:T(8,128)(2,1)} %get-tuple-element.88) | copy-start | bytes 393220
  444.6 4.9 %copy-start.8 = (bf16[8,128,2048]{2,1,0:T(8,128)(2,1)S(1)}, bf16[8,128,2048]{2,1,0:T(8,128)(2,1)}, u32[]{:S(2)}) copy-start(bf16[8,128,2048]{2,1,0:T(8,128)(2,1)} %get-tuple-element.25) | copy-start | bytes 12582916
  (5 other events, 8.3 us)

commit v2 on v0

v2 whole, which is shorter than its diff:
```python
import math

import jax
import jax.numpy as jnp
import numpy as np
from jax import lax
from jax.experimental import pallas as pl
from jax.experimental.pallas import tpu as pltpu
from jax.sharding import PartitionSpec as P

EPSILON = 1e-05
NEGATIVE = -1e30
SCALE = 1.0 / math.sqrt(128)
MESH = pl.DeviceIdType.MESH
F32, BF16 = jnp.float32, jnp.bfloat16
VM = pl.BlockSpec(memory_space=pltpu.VMEM)
ANY = pl.BlockSpec(memory_space=pl.ANY)
NN, NT, TN = ((1,), (0,)), ((1,), (1,)), ((0,), (0,))
LO, HI = pl.ds(0, 64), pl.ds(64, 64)


def dot(a, b, dims=NN):
    return lax.dot_general(a, b, (dims, ((), ())), preferred_element_type=F32)


def loop(count, body):
    def one(i, carry):
        body(i)
        return carry

    lax.fori_loop(0, count, one, 0)


def rows(i, step):
    return pl.ds(pl.multiple_of(i * step, step), step)


class Links:
    def __init__(self, send, recv):
        dp, t = lax.axis_index("dp"), lax.axis_index("tensor")
        self.dp, self.t = dp, t
        self.x, self.y, self.z, self.c = dp // 4, dp % 4, t // 2, t % 2
        self.send, self.recv, self.used = send, recv, 0

    def slot(self, d, c=None):
        return 2 * ((self.z + d) % 4) + (self.c if c is None else c)

    def zdev(self, d):
        return (self.dp, self.slot(d))

    def sib(self):
        return (self.dp, self.slot(0, 1 - self.c))

    def xdev(self, d):
        return (((self.x + d) % 4) * 4 + self.y, self.t)

    def ydev(self, d):
        return (self.x * 4 + (self.y + d) % 4, self.t)

    def barrier(self, devs):
        b = pltpu.get_barrier_semaphore()
        for dev in devs:
            pl.semaphore_signal(b, inc=1, device_id=dev, device_id_type=MESH)
        pl.semaphore_wait(b, len(devs))

    def take(self, n=1):
        at = self.used
        self.used += n
        return at

    def copy(self, at, src, dst, dev):
        return pltpu.make_async_remote_copy(
            src_ref=src,
            dst_ref=dst,
            send_sem=self.send.at[at],
            recv_sem=self.recv.at[at],
            device_id=dev,
            device_id_type=MESH,
        )

    def go(self, src, dst, dev):
        copy = self.copy(self.take(), src, dst, dev)
        copy.start()
        return copy


HOPS = ("h1", "h2", "u1", "u2", "w1", "w2")


class ReduceZ:
    def __init__(self, k, part, rc, hp, hm, fp, fm):
        self.k, self.part, self.rc = k, part, rc
        self.hp, self.hm, self.fp, self.fm = hp, hm, fp, fm
        self.base = k.take(10)

    def _swap(self, d):
        k = self.k
        return k.copy(self.base + d, self.part.at[k.slot(d, 1 - k.c)], self.rc.at[d], k.sib())

    def swap(self, d):
        self._swap(d).start()

    def core_add(self, d):
        self._swap(d).wait_recv()
        mine = self.part.at[self.k.slot(d)]

        def body(i):
            s = rows(i, 32)
            mine[s] = mine[s] + self.rc[d, s]

        loop(4, body)

    def hop(self, name):
        k, p = self.k, self.part
        up, down = k.zdev(1), k.zdev(-1)
        src, dst, dev = {
            "h1": (p.at[k.slot(2), LO], self.hp, up),
            "h2": (p.at[k.slot(2), HI], self.hm, down),
            "u1": (p.at[k.slot(1), HI], self.fp.at[HI], up),
            "u2": (p.at[k.slot(3), LO], self.fm.at[LO], down),
            "w1": (p.at[k.slot(1), LO], self.fp.at[LO], up),
            "w2": (p.at[k.slot(3), HI], self.fm.at[HI], down),
        }[name]
        return k.copy(self.base + 4 + HOPS.index(name), src, dst, dev)

    def send(self, *names):
        for name in names:
            self.hop(name).start()

    def mid(self):
        k, p = self.k, self.part
        self.hop("h1").wait_recv()
        p[k.slot(1), LO] = p[k.slot(1), LO] + self.hp[...]
        self.send("w1")
        self.hop("h2").wait_recv()
        p[k.slot(3), HI] = p[k.slot(3), HI] + self.hm[...]
        self.send("w2")

    def finish(self):
        for name in ("u1", "u2", "w1", "w2"):
            self.hop(name).wait_recv()

    def own(self, s):
        mine = self.part[self.k.slot(0), s].astype(F32)
        return mine + self.fp[s].astype(F32) + self.fm[s].astype(F32)

    def drain(self):
        for d in range(4):
            self._swap(d).wait_send()
        for name in HOPS:
            self.hop(name).wait_send()


class GatherZ:
    def __init__(self, k, dst, own):
        self.k, self.dst, self.own = k, dst, own
        at = k.take(9)
        self.at = {name: at + i for i, name in enumerate(("a1", "b1", "a2", "b2", "s0", "f1", "f2", "s1", "s2"))}
        self.at["s3"] = k.take()

    def c(self, name):
        k, dst, own = self.k, self.dst, self.own
        me, below, above, far = k.t, k.slot(-1), k.slot(1), k.slot(2)
        up, down, sib = k.zdev(1), k.zdev(-1), k.sib()
        src, to, dev = {
            "a1": (own.at[LO], dst.at[me, LO], up),
            "b1": (own.at[HI], dst.at[me, HI], down),
            "a2": (own.at[HI], dst.at[me, HI], up),
            "b2": (own.at[LO], dst.at[me, LO], down),
            "s0": (own, dst.at[me], sib),
            "f1": (dst.at[below, LO], dst.at[below, LO], up),
            "f2": (dst.at[above, HI], dst.at[above, HI], down),
            "s1": (dst.at[below], dst.at[below], sib),
            "s2": (dst.at[above], dst.at[above], sib),
            "s3": (dst.at[far], dst.at[far], sib),
        }[name]
        return k.copy(self.at[name], src, to, dev)

    def start(self):
        for name in ("a1", "b1", "a2", "b2", "s0"):
            self.c(name).start()

    def forward(self):
        self.c("a1").wait_recv()
        self.c("f1").start()
        self.c("b1").wait_recv()
        self.c("f2").start()

    def share_near(self):
        self.c("b2").wait_recv()
        self.c("s2").start()
        self.c("a2").wait_recv()
        self.c("s1").start()

    def share_far(self):
        self.c("f1").wait_recv()
        self.c("f2").wait_recv()
        self.c("s3").start()

    def ready(self, d):
        self.c({0: "s0", 1: "s2", 3: "s1", 2: "s3"}[d]).wait_recv()

    def drain(self):
        for name in self.at:
            self.c(name).wait_send()


def ring4(k, view, hp, hm, fp, fm, dev, half, add, fin, sent):
    h1 = k.go(view(2, 0), hp, dev(1))
    h2 = k.go(view(2, 1), hm, dev(-1))
    u1 = k.go(view(1, 1), half(fp, 1), dev(1))
    u2 = k.go(view(3, 0), half(fm, 0), dev(-1))
    yield
    h1.wait_recv()
    add(view(1, 0), hp)
    w1 = k.go(view(1, 0), half(fp, 0), dev(1))
    h2.wait_recv()
    add(view(3, 1), hm)
    w2 = k.go(view(3, 1), half(fm, 1), dev(-1))
    sent.extend((h1, h2, u1, u2, w1, w2))
    yield
    for copy in (u1, w1, u2, w2):
        copy.wait_recv()
    fin()


def grads_xy(k, g, bufs, store, sent):
    R = g.shape[2]
    H, Q = R // 2, R // 4
    (hp1, hm1, fp1, fm1, hp2, hm2, fp2, fm2, tp1, tm1, tq1, tr1, tp2, tm2, tq2, tr2) = bufs
    first, second = pl.ds(0, H), pl.ds(H, H)

    def wide_half(f, h):
        return f.at[pl.ds(2 * h, 2)]

    def wide_add(dst, src):
        loop(2, lambda i: dst.__setitem__(i, dst[i] + src[i]))

    def wide_fin(own, fp, fm):
        def body(i):
            o = own(i)
            o[...] = (o[...].astype(F32) + fp[i].astype(F32) + fm[i].astype(F32)).astype(BF16)

        return lambda: loop(4, body)

    def thin_half(f, h):
        return f.at[pl.ds(Q * h, Q)]

    def thin_add(dst, src):
        dst[...] = dst[...] + src[...]

    a = ring4(
        k, lambda d, h: g.at[(k.x + d) % 4, pl.ds(2 * h, 2), first],
        hp1, hm1, fp1, fm1, k.xdev, wide_half, wide_add,
        wide_fin(lambda i: g.at[k.x, i, first], fp1, fm1), sent,
    )
    b = ring4(
        k, lambda d, h: g.at[pl.ds(2 * h, 2), (k.y + d) % 4, second],
        hp2, hm2, fp2, fm2, k.ydev, wide_half, wide_add,
        wide_fin(lambda i: g.at[i, k.y, second], fp2, fm2), sent,
    )
    next(a); next(b)
    yield
    next(a); next(b)
    yield
    for _ in a:
        pass
    for _ in b:
        pass

    def thin_fin(own, fp, fm, at):
        def fin():
            store(at, H, own[...].astype(F32) + fp[...].astype(F32) + fm[...].astype(F32))

        return fin

    a = ring4(
        k, lambda d, h: g.at[k.x, (k.y + d) % 4, pl.ds(Q * h, Q)],
        tp1, tm1, tq1, tr1, k.ydev, thin_half, thin_add,
        thin_fin(g.at[k.x, k.y, first], tq1, tr1, 0), sent,
    )
    b = ring4(
        k, lambda d, h: g.at[(k.x + d) % 4, k.y, pl.ds(H + Q * h, Q)],
        tp2, tm2, tq2, tr2, k.xdev, thin_half, thin_add,
        thin_fin(g.at[k.x, k.y, second], tq2, tr2, H), sent,
    )
    next(a); next(b)
    yield
    next(a); next(b)
    yield
    for _ in a:
        pass
    for _ in b:
        pass


def grads_bufs(R):
    H, Q = R // 2, R // 4
    b = lambda *s: pltpu.VMEM(s, BF16)
    wide = [b(2, H, 128), b(2, H, 128), b(4, H, 128), b(4, H, 128)]
    thin = [b(Q, 128), b(Q, 128), b(H, 128), b(H, 128)]
    return wide + wide + thin + thin


def unit(values):
    factor = lax.rsqrt(jnp.mean(values * values, axis=-1, keepdims=True) + EPSILON)
    return values * factor, factor


def norm_back(d_normed, gain, normed, factor):
    scaled = d_normed * gain
    return factor * (scaled - normed * jnp.mean(scaled * normed, axis=-1, keepdims=True))


def turn(values, cos, sin):
    return values * cos + pltpu.roll(values, 64, axis=1) * sin


NSEM = 256
NAMES = (
    "x", "oc", "wq", "wkv", "wo", "wg", "wu", "wd", "kvct", "cs", "gain1", "gain2", "lens", "out", "ig",
    "kvo", "gsum", "kvsum", "n1h", "ph", "XB", "N2", "OC", "PA", "PB", "RC", "hp", "hm", "fp", "fm",
    "hp2", "hm2", "fp2", "fm2", "h1", "dh1", "xs", "stage2", "wqkv", "wov", "q", "kv",
    "att", "dq", "dkv", "csv", "hid", "dg", "du", "gn", "kvb", "kvr", "kvi", "dkvs",
    "kvrc", "kvz", "kvx", "kvy", "kvct_v", "free_a", "free_b", "free_rc", "lsem", "send", "recv",
)


def rope_rows(lens, csv):
    low = lax.broadcasted_iota(jnp.int32, (1, 128), 1) < 64
    starts = [jnp.int32(0)]
    for doc in range(3):
        starts.append(starts[-1] + lens[0, doc])

    def look(i, found):
        s = rows(i, 256)
        place = lax.broadcasted_iota(jnp.int32, (256, 128), 0) + s.start
        table = csv[s, 0:128]
        return tuple(
            f + jnp.sum(jnp.where(place == start, table, 0.0), axis=0, keepdims=True)
            for f, start in zip(found, starts)
        )

    first = starts
    found = lax.fori_loop(0, 4, look, (jnp.zeros((1, 128), F32),) * 4)
    turned = [pltpu.roll(row, 64, axis=1) for row in found]
    a = [jnp.where(low, row, other) for row, other in zip(found, turned)]
    b = [jnp.where(low, other, -row) for row, other in zip(found, turned)]

    def body(i):
        s = rows(i, 256)
        place = lax.broadcasted_iota(jnp.int32, (256, 128), 0) + s.start
        here, aa, bb = jnp.zeros((256, 128), jnp.int32), a[0], b[0]
        for doc in (1, 2, 3):
            later = place >= first[doc]
            here = jnp.where(later, first[doc], here)
            aa = jnp.where(later, a[doc], aa)
            bb = jnp.where(later, b[doc], bb)
        table = csv[s, 0:128]
        both = table * aa + pltpu.roll(table, 64, axis=1) * bb
        other = pltpu.roll(both, 64, axis=1)
        csv[s, 0:128] = jnp.where(low, both, other)
        csv[s, 128:256] = jnp.where(low, -other, both)
        csv[s, 256:384] = here.astype(F32)

    loop(4, body)


def finish(out, ig, kvo, gsum, out_f, ig_f, kv_f, gq, go, gg, gu, gd, query, sem):
    copies = []

    def copy(src, dst):
        copies.append(pltpu.make_async_copy(src, dst, sem.at[len(copies)]))
        copies[-1].start()

    copy(gsum.at[pl.ds(2368, 256)], query)
    for i in range(4):
        s = pl.ds(256 * i, 256)
        copy(out.at[s], out_f.at[s])
        copy(ig.at[s], ig_f.at[s])
    copy(kvo, kv_f)
    copy(gsum.at[pl.ds(2112, 256)], go)
    copy(gsum.at[pl.ds(704, 704)], gg)
    copy(gsum.at[pl.ds(1408, 704)], gu)
    copy(gsum.at[pl.ds(0, 704)], gd)
    copies[0].wait()
    gq[...] = query[...].T
    for item in copies[1:]:
        item.wait()


def block(*refs):
    r = dict(zip(NAMES, refs))
    rest = refs[len(NAMES):]
    bufs_a, bufs_b = rest[0:16], rest[16:32]
    R = type("R", (), r)
    lsem = R.lsem
    k = Links(R.send, R.recv)
    XB, N2, OC, PA, PB = R.XB, R.N2, R.OC, R.PA, R.PB
    uses = [0]

    def local(src, dst):
        copy = pltpu.make_async_copy(src, dst, lsem.at[uses[0]])
        uses[0] += 1
        copy.start()
        return copy

    ld_x = local(R.x, XB)
    ld_q = local(R.wq, R.wqkv.at[:, pl.ds(0, 256)])
    ld_kv = local(R.wkv, R.wqkv.at[:, pl.ds(256, 256)])
    ld_cs = local(R.cs, R.csv.at[:, pl.ds(0, 128)])
    ld_wo = local(R.wo, R.wov)
    ld_oc = local(R.oc, OC)
    ld_ct = local(R.kvct.at[k.t], R.kvct_v)
    k.barrier(
        [k.zdev(1), k.zdev(-1), k.zdev(2), k.sib()]
        + [dev(d) for dev in (k.xdev, k.ydev) for d in (1, 2, 3)]
    )

    ld_x.wait()
    R.xs[...] = XB[k.t]

    def norm1(i):
        t, s = i // 2, rows(i % 2, 64)
        XB[t, s] = (unit(XB[t, s].astype(F32))[0] * R.gain1[...]).astype(BF16)

    loop(16, norm1)
    st_n1 = local(XB, R.n1h)
    ld_cs.wait()
    rope_rows(R.lens, R.csv)
    ld_q.wait()
    ld_kv.wait()

    def project(i):
        s = rows(i, 256)
        pre = dot(XB[pl.ds(2 * i, 2)].reshape(256, 2048), R.wqkv[...])
        cos, sin = R.csv[s, 0:128], R.csv[s, 128:256]
        for h in range(2):
            R.q[s, 128 * h:128 * h + 128] = turn(pre[:, 128 * h:128 * h + 128], cos, sin).astype(BF16)
        R.kv[s, 0:128] = turn(pre[:, 256:384], cos, sin).astype(BF16)
        R.kv[s, 128:256] = pre[:, 384:512].astype(BF16)

    loop(4, project)
    st_kv = local(R.kv, R.kvo)
    ld_wo.wait()

    def back_rows(j):
        return pl.ds(pl.multiple_of((j // 2) * (j - 2) * 256, 256), 768)

    rs = ReduceZ(k, PA, R.RC, R.hp, R.hm, R.fp, R.fm)

    def attend(i):
        d = (2 - i + 3 * (i // 2) - 2 * (i // 3)) % 4
        j = (k.z + d) % 4
        s, ks = rows(j, 256), back_rows(j)
        kk, vv = R.kv[ks, 0:128], R.kv[ks, 128:256]
        col = lax.broadcasted_iota(jnp.int32, (256, 768), 1) + ks.start
        row = lax.broadcasted_iota(jnp.int32, (256, 768), 0) + s.start
        first = R.csv[s, 256:384][:, 0:1].astype(jnp.int32)
        bias = jnp.where((col <= row) & (col >= first), 0.0, NEGATIVE)
        done = []
        for h in range(2):
            sc = dot(R.q[s, 128 * h:128 * h + 128], kk, NT) * SCALE + bias
            grown = jnp.exp(sc - jnp.max(sc, axis=-1, keepdims=True))
            probs = (grown * (1.0 / jnp.sum(grown, axis=-1, keepdims=True))).astype(BF16)
            PB[pl.ds(2 * j, 2), :, 768 * h:768 * h + 768] = probs.reshape(2, 128, 768)
            done.append(dot(probs, vv).astype(BF16))
        mixed = jnp.concatenate(done, axis=1)
        R.att[s] = mixed
        PA[pl.ds(2 * j, 2)] = dot(mixed, R.wov[...]).astype(BF16).reshape(2, 128, 2048)
        rs.swap(d)

        @pl.when(i == 1)
        def _():
            rs.core_add(2)
            rs.send("h1", "h2")

        @pl.when(i == 2)
        def _():
            rs.core_add(1)
            rs.send("u1")

        @pl.when(i == 3)
        def _():
            rs.core_add(3)
            rs.send("u2")

    loop(4, attend)
    st_p = local(PB.at[:, :, pl.ds(0, 1536)], R.ph)
    rs.core_add(0)
    rs.mid()
    g2 = GatherZ(k, N2, N2.at[k.t])
    dn = ReduceZ(k, PA, R.RC, R.hp, R.hm, R.fp, R.fm)
    ou = ReduceZ(k, PB, R.RC, R.hp2, R.hm2, R.fp2, R.fm2)
    gd = GatherZ(k, XB, XB.at[k.t])

    def mlp(wgv, wuv, wdv, wsem):
        lg = pltpu.make_async_copy(R.wg, wgv, wsem.at[0])
        lu = pltpu.make_async_copy(R.wu, wuv, wsem.at[1])
        ld = pltpu.make_async_copy(R.wd, wdv, wsem.at[2])
        ld.start()
        lg.start()
        lu.start()
        ld_oc.wait()
        ld.wait()

        def early(i):
            R.du[rows(i, 256)] = dot(OC[pl.ds(2 * i, 2)].reshape(256, 2048), wdv[...], NT).astype(BF16)

        loop(4, early)
        rs.finish()

        def shard1(i):
            s = rows(i, 32)
            h1 = R.xs[s].astype(F32) + rs.own(s)
            R.h1[s] = h1
            N2[k.t, s] = (unit(h1)[0] * R.gain2[...]).astype(BF16)

        loop(4, shard1)
        g2.start()
        rs.drain()
        lg.wait()
        lu.wait()
        st_n1.wait()
        st_p.wait()

        def chunk(i):
            d = i + i // 2 - 2 * (i // 3)
            j = (k.z + d) % 4
            s = rows(j, 256)

            @pl.when(i == 0)
            def _():
                g2.ready(0)

            @pl.when(i == 1)
            def _():
                g2.forward()
                g2.share_near()
                g2.ready(1)

            @pl.when(i == 2)
            def _():
                g2.ready(3)

            @pl.when(i == 3)
            def _():
                g2.share_far()
                g2.ready(2)

            n2 = N2[pl.ds(2 * j, 2)].reshape(256, 2048)
            gate = dot(n2, wgv[...], NT)
            up = dot(n2, wuv[...], NT)
            sig = 1.0 / (1.0 + jnp.exp(-gate))
            silu = gate * sig
            R.hid[s] = (silu * up).astype(BF16)
            dh = R.du[s].astype(F32)
            dg = (dh * up * sig * (1.0 + gate * (1.0 - sig))).astype(BF16)
            du = (dh * silu).astype(BF16)
            R.dg[s] = dg
            R.du[s] = du

            def cols(n):
                w = rows(n, 512)
                part = dot(R.dg[s], wgv[:, w]) + dot(R.du[s], wuv[:, w])
                PA[pl.ds(2 * j, 2), :, w] = part.astype(BF16).reshape(2, 128, 512)

            loop(4, cols)
            dn.swap(d)

            @pl.when(i == 1)
            def _():
                dn.core_add(0)

            @pl.when(i == 2)
            def _():
                dn.core_add(1)
                dn.send("u1")

            @pl.when(i == 3)
            def _():
                dn.core_add(3)
                dn.send("u2")

        loop(4, chunk)

        dn.core_add(2)
        dn.send("h1", "h2")

        def out_part(i):
            PB[pl.ds(2 * i, 2)] = dot(R.hid[rows(i, 256)], wdv[...]).astype(BF16).reshape(2, 128, 2048)

        loop(4, out_part)

    pl.run_scoped(
        mlp, b16(704, 2048), b16(704, 2048), b16(704, 2048),
        pltpu.SemaphoreType.DMA((3,)),
    )
    g2.drain()
    dn.mid()

    def weights(gm):
        sent_a, sent_b, sent_c, sent_d = [], [], [], []

        def grad(lhs, first, count, at, to, rhs):
            def body(n):
                left = lhs[:, first:first + count]
                res = dot(left, rhs[:, :, rows(n, 256)].reshape(1024, 256), TN).astype(BF16)
                for half in range(2):
                    e = 2 * n + half
                    at[e // 4, e % 4, to:to + count] = res[:, 128 * half:128 * half + 128]

            loop(8, body)

        def keep(offset):
            def store(at, count, value):
                R.gsum[offset + at:offset + at + count] = value

            return store

        grad(R.hid, 0, 704, gm.at[0], 0, OC)
        xy_down = grads_xy(k, gm.at[0], bufs_a, keep(0), sent_a)
        next(xy_down, None)
        ld_p = local(R.ph, OC.at[:, :, pl.ds(0, 1536)])
        dn.finish()
        R.gn[...] = jnp.zeros_like(R.gn)

        def shard2(i):
            s = rows(i, 32)
            d = dn.own(s)
            y2, r2 = unit(R.h1[s])
            dh1 = R.stage2[s].astype(F32) + norm_back(d, R.gain2[...], y2, r2)
            R.dh1[s] = dh1
            XB[k.t, s] = dh1.astype(BF16)
            dy = d * y2
            R.gn[0] += dy[0:8] + dy[8:16] + dy[16:24] + dy[24:32]

        loop(4, shard2)
        gd.start()
        dn.drain()
        grad(R.dg, 0, 704, gm.at[1], 0, N2)
        xy_gate = grads_xy(k, gm.at[1], bufs_b, keep(704), sent_b)
        next(xy_gate, None)
        next(xy_down, None)
        gd.ready(0)
        for d in range(4):
            ou.swap(d)
        gd.forward()
        grad(R.du, 0, 704, gm.at[2], 0, N2)
        for d in range(4):
            ou.core_add(d)
        ou.send("h1", "h2", "u1", "u2")
        pl.semaphore_signal(R.free_rc, inc=1, device_id=k.sib(), device_id_type=MESH)
        gd.share_near()
        next(xy_down, None)
        next(xy_gate, None)
        ld_p.wait()
        rn = ReduceZ(k, PA, R.RC, R.hp, R.hm, R.fp, R.fm)
        pl.semaphore_wait(R.free_rc, 1)
        R.dkv[...] = jnp.zeros_like(R.dkv)

        def back(i):
            d = i + i // 2 - 2 * (i // 3)
            j = (k.z + d) % 4
            s, ks = rows(j, 256), back_rows(j)

            @pl.when(i == 1)
            def _():
                gd.ready(1)

            @pl.when(i == 2)
            def _():
                gd.ready(3)

            @pl.when(i == 3)
            def _():
                gd.share_far()
                gd.ready(2)

            da = dot(XB[pl.ds(2 * j, 2)].reshape(256, 2048), R.wov[...], NT).astype(BF16)
            kk, vv = R.kv[ks, 0:128], R.kv[ks, 128:256]
            cos, sin = R.csv[s, 0:128], R.csv[s, 128:256]
            done = []
            for h in range(2):
                lanes = slice(128 * h, 128 * h + 128)
                probs = OC[pl.ds(2 * j, 2), :, 768 * h:768 * h + 768].reshape(256, 768)
                wide = probs.astype(F32)
                dp = dot(da[:, lanes], vv, NT)
                ds = (wide * (dp - jnp.sum(wide * dp, axis=-1, keepdims=True))).astype(BF16)
                done.append(turn(dot(ds, kk) * SCALE, cos, -sin).astype(BF16))
                R.dkv[ks, 0:128] += dot(ds, R.q[s, lanes], TN) * SCALE
                R.dkv[ks, 128:256] += dot(probs, da[:, lanes], TN)
            dq = jnp.concatenate(done, axis=1)
            R.dq[s] = dq
            PA[pl.ds(2 * j, 2)] = dot(dq, R.wqkv[:, 0:256], NT).astype(BF16).reshape(2, 128, 2048)
            rn.swap(d)

            @pl.when(i == 1)
            def _():
                rn.core_add(0)

            @pl.when(i == 2)
            def _():
                rn.core_add(1)
                rn.send("u1")

            @pl.when(i == 3)
            def _():
                rn.core_add(3)
                rn.send("u2")

        loop(4, back)
        rn.core_add(2)
        rn.send("h1", "h2")
        for d in range(4):
            for c in range(2):
                R.kvb[c, d] = R.dkv[(2 * d + c) * 128:(2 * d + c) * 128 + 128].astype(BF16)
        kv_swap = k.go(R.kvb.at[1 - k.c], R.kvr, k.sib())
        ld_n1 = local(R.n1h, OC)
        ou.mid()
        for _ in xy_down:
            pass
        next(xy_gate, None)

        def hand_over(sent, free):
            for dev in (k.xdev(1), k.xdev(-1), k.ydev(1), k.ydev(-1)):
                pl.semaphore_signal(free, inc=1, device_id=dev, device_id_type=MESH)
            for copy in sent:
                copy.wait_send()
            pl.semaphore_wait(free, 4)

        hand_over(sent_a, R.free_a)
        xy_up = grads_xy(k, gm.at[2], bufs_a, keep(1408), sent_c)
        next(xy_up, None)
        rn.mid()
        kv_swap.wait_recv()
        R.kvb[k.c] = R.kvb[k.c] + R.kvr[...]
        kv_in = [k.go(R.kvb.at[k.c, (k.z + d) % 4], R.kvi.at[d - 1], k.zdev(d)) for d in (1, 2, 3)]
        gat = gm.at[0, :, :, pl.ds(0, 512)]
        grad(R.att, 0, 256, gat, 0, XB)
        next(xy_gate, None)
        next(xy_up, None)
        ld_n1.wait()
        grad(R.dq, 0, 256, gat, 256, OC)
        for _ in xy_gate:
            pass
        hand_over(sent_b, R.free_b)

        def part(buf, n):
            return buf.at[:, pl.ds(0, n)] if len(buf.shape) == 3 else buf.at[pl.ds(0, n)]

        sizes = [256] * 8 + [128, 128, 256, 256] * 2
        bufs_c = [part(buf, n) for buf, n in zip(bufs_b, sizes)]
        xy_att = grads_xy(k, gat, bufs_c, keep(2112), sent_d)
        next(xy_att, None)
        next(xy_up, None)
        for copy in kv_in:
            copy.wait_recv()
        ld_ct.wait()
        total = R.kvb[k.c, k.z].astype(F32) + R.kvct_v[...]
        for d in range(3):
            total = total + R.kvi[d].astype(F32)
        own = rows(k.t, 128)
        cos, sin = R.csv[own, 0:128], R.csv[own, 128:256]
        R.dkvs[:, 0:128] = turn(total[:, 0:128], cos, -sin).astype(BF16)
        R.dkvs[:, 128:256] = total[:, 128:256].astype(BF16)
        rn.finish()
        gi = GatherZ(k, R.ig, R.xs)

        def shard3(i):
            s = rows(i, 32)
            d = rn.own(s) + dot(R.dkvs[s], R.wqkv[:, 256:512], NT)
            y1, r1 = unit(R.xs[s].astype(F32))
            R.xs[s] = (R.dh1[s] + norm_back(d, R.gain1[...], y1, r1)).astype(BF16)
            XB[k.t, s] = (y1 * R.gain1[...]).astype(BF16)
            dy = d * y1
            R.gn[1] += dy[0:8] + dy[8:16] + dy[16:24] + dy[24:32]

        gd.drain()
        R.gn[1] = jnp.zeros((8, 2048), F32)
        loop(4, shard3)
        gi.start()
        st_ig = local(R.xs, R.ig.at[k.t])
        ou.finish()

        def shard4(i):
            s = rows(i, 32)
            R.stage2[s] = (R.h1[s] + ou.own(s)).astype(BF16)

        loop(4, shard4)
        go = GatherZ(k, R.out, R.stage2)
        go.start()
        st_out = local(R.stage2, R.out.at[k.t])
        small = dot(XB[k.t], R.dkvs[...], TN)
        tops = [jnp.broadcast_to(jnp.sum(R.gn[i], axis=0, keepdims=True), (64, 2048)) for i in (1, 0)]
        small = jnp.concatenate([small, jnp.concatenate(tops, axis=0).T], axis=1).astype(BF16)
        sm = gm.at[1]
        for e in range(128):
            dp, at = e // 8, 48 * ((e % 2) * 4 + (e % 8) // 2)
            for n in range(3):
                sm[dp // 4, dp % 4, at + 16 * n:at + 16 * n + 16] = small[16 * e:16 * e + 16, 128 * n:128 * n + 128]
        sm_swap = k.go(sm.at[:, :, pl.ds(192 * (1 - k.c), 192)], R.kvrc, k.sib())
        next(xy_att, None)
        next(xy_up, None)
        gi.forward()
        sm_swap.wait_recv()
        for e in range(16):
            at = sm.at[e // 4, e % 4, pl.ds(192 * k.c, 192)]
            at[...] = at[...] + R.kvrc[e // 4, e % 4]
        mine = lambda d: sm.at[:, :, pl.ds(192 * k.c + 48 * ((k.z + d) % 4), 48)]
        z_in = [k.go(mine(d), R.kvz.at[d - 1], k.zdev(d)) for d in (1, 2, 3)]
        next(xy_att, None)
        next(xy_up, None)
        for copy in z_in:
            copy.wait_recv()
        R.kvz[3] = (mine(0)[...].astype(F32) + sum(R.kvz[i].astype(F32) for i in range(3))).astype(BF16)
        x_in = [k.go(R.kvz.at[3, (k.x + d) % 4], R.kvx.at[d - 1], k.xdev(d)) for d in (1, 2, 3)]
        gi.share_near()
        go.forward()
        go.share_near()
        for copy in x_in:
            copy.wait_recv()
        R.kvx[3] = (
            R.kvz[3, k.x].astype(F32) + sum(R.kvx[i].astype(F32) for i in range(3))
        ).astype(BF16)
        y_in = [k.go(R.kvx.at[3, (k.y + d) % 4], R.kvy.at[d - 1], k.ydev(d)) for d in (1, 2, 3)]
        next(xy_att, None)
        next(xy_up, None)
        for copy in y_in:
            copy.wait_recv()
        whole = R.kvx[3, k.y].astype(F32) + sum(R.kvy[i].astype(F32) for i in range(3))
        for n in range(3):
            R.kvsum[:, 128 * n:128 * n + 128] = whole[16 * n:16 * n + 16]
        gi.share_far()
        for xy in (xy_att, xy_up):
            for _ in xy:
                pass
        go.share_far()
        for ag in (gi, go):
            for d in (0, 1, 3, 2):
                ag.ready(d)
        for copy in sent_c + sent_d + kv_in + z_in + x_in + y_in + [kv_swap, sm_swap]:
            copy.wait_send()
        for item in (rn, ou, gi, go):
            item.drain()
        st_ig.wait()
        st_out.wait()

    R.stage2[...] = OC[k.t]
    pl.run_scoped(weights, pltpu.VMEM((3, 4, 4, 704, 128), BF16))
    st_kv.wait()


def b16(*s):
    return pltpu.VMEM(s, BF16)


def b32(*s):
    return pltpu.VMEM(s, F32)


def angle_table():
    inverse = np.exp(np.arange(64) * (-2.0 * math.log(10000.0) / 128))
    angle = np.arange(1024)[:, None] * inverse
    return np.concatenate([np.cos(angle), np.sin(angle)], axis=1).astype(np.float32)


def per_device(
    inputs, doc_lengths, norm1_gain, w_query, w_shared_kv, w_output, norm2_gain,
    w_gate, w_up, w_down, out_cotangent, kv_cotangent,
):
    cut = lambda v: v.reshape(8, 128, v.shape[-1])
    ins = [
        cut(inputs), cut(out_cotangent), w_query, w_shared_kv, w_output, w_gate.T, w_up.T, w_down,
        cut(kv_cotangent), jnp.asarray(angle_table()), norm1_gain.reshape(1, 2048), norm2_gain.reshape(1, 2048),
        doc_lengths,
    ]
    wide = ((8, 128, 2048), BF16)
    outs = [
        wide, wide, ((1024, 256), BF16), ((2624, 128), F32), ((16, 384), F32), wide, ((8, 128, 1536), BF16),
    ]
    big = b16(8, 128, 2048)
    hops = [b16(64, 2048), b16(64, 2048), b16(128, 2048), b16(128, 2048)]
    core = b16(4, 128, 2048)
    scratch = (
        [big] * 5 + [core] + hops + hops
        + [b32(128, 2048), b32(128, 2048), b16(128, 2048), b16(128, 2048)]
        + [b16(2048, 512), b16(256, 2048), b16(1024, 256), b16(1024, 256), b16(1024, 256), b16(1024, 256)]
        + [b32(1024, 256), b32(1024, 384), b16(1024, 704), b16(1024, 704), b16(1024, 704), b32(2, 8, 2048)]
        + [b16(2, 4, 128, 256), b16(4, 128, 256), b16(3, 128, 256), b16(128, 256)]
        + [b16(4, 4, 192, 128), b16(4, 4, 4, 48, 128), b16(4, 4, 48, 128), b16(3, 48, 128)]
        + [b32(128, 256), pltpu.SemaphoreType.REGULAR] + [pltpu.SemaphoreType.REGULAR] * 2 + [pltpu.SemaphoreType.DMA((16,))]
        + [pltpu.SemaphoreType.DMA((NSEM,)), pltpu.SemaphoreType.DMA((NSEM,))]
        + grads_bufs(704) + grads_bufs(704)
    )
    output, input_grad, shared_kv, gsum, kvsum, _, _ = pl.pallas_call(
        block,
        out_shape=[jax.ShapeDtypeStruct(s, d) for s, d in outs],
        in_specs=[ANY] * 10 + [VM] * 2 + [pl.BlockSpec(memory_space=pltpu.SMEM)],
        out_specs=[ANY] * 3 + [VM] * 2 + [ANY] * 2,
        scratch_shapes=scratch,
        compiler_params=pltpu.CompilerParams(
            collective_id=0, has_side_effects=True, vmem_limit_bytes=VLIM
        ),
    )(*ins)
    shapes = [
        ((1024, 2048), BF16), ((1024, 2048), BF16), ((1024, 256), BF16), ((128, 256), F32), ((256, 128), F32),
        ((704, 128), F32), ((704, 128), F32), ((704, 128), F32),
    ]
    flat = lambda v: v.reshape(1024, 2048)
    output, input_grad, shared_kv, g_query, g_out, g_gate, g_up, g_down = pl.pallas_call(
        finish,
        out_shape=[jax.ShapeDtypeStruct(s, d) for s, d in shapes],
        in_specs=[ANY] * 4,
        out_specs=[ANY] * 3 + [VM] + [ANY] * 4,
        scratch_shapes=[b32(256, 128), pltpu.SemaphoreType.DMA((14,))],
        compiler_params=pltpu.CompilerParams(vmem_limit_bytes=8 * 2**20),
    )(flat(output), flat(input_grad), shared_kv, gsum)
    return (
        output, input_grad, shared_kv, kvsum[:, 256], g_query, kvsum[:, 0:256], g_out, kvsum[:, 320],
        g_gate.T, g_up.T, g_down,
    )


VLIM = 63 * 2**20


def solution(mesh):
    placed = (
        P("dp", None), P("dp", None), P(), P(None, "tensor"), P(), P("tensor", None), P(),
        P(None, "tensor"), P(None, "tensor"), P("tensor", None), P("dp", None), P("dp", None),
    )
    return jax.shard_map(
        per_device,
        mesh=mesh,
        in_specs=placed,
        out_specs=(
            P("dp", None), P("dp", None), P("dp", None), P(("dp", "tensor")), P("dp", "tensor"),
            P(("dp", "tensor"), None), P("tensor", "dp"), P(("dp", "tensor")), P("dp", "tensor"),
            P("dp", "tensor"), P("tensor", "dp"),
        ),
        check_vma=False,
    )
```

time: 1560 us -> 222 us (0.14)
  waiting for transfers between devices: 1270 us -> 0 us
  Pallas kernels: 0 us -> 213 us
  matrix products: 99.3 us -> 0 us
  other arithmetic: 68.3 us -> 0 us
  blocking collectives: 67.1 us -> 0 us
  local copies, waits for them, and re-layouts: 30.5 us -> 8.04 us
    reduce_scatter x2 -> x0, waiting for transfers between devices: 614 us -> none  [the longest x1 540 us: per_device(): lax.psum_scatter(grad_kv, ('dp', 'tensor'), scatter_dimension=0, tiled=True)]
    psum x3 -> x0, waiting for transfers between devices: 358 us -> none  [tensor_total(): return lax.psum(values, 'tensor')]
    unnamed x13 -> x0, waiting for transfers between devices: 297 us -> none
    pallas_call x0 -> x2, Pallas kernels: none -> 213 us  [the longest x1 208 us: per_device(): pl.pallas_call(block, out_shape=[jax.ShapeDtypeStruct(s, d) for s, d in o...]
    dot_general x24 -> x0, matrix products: 99.3 us -> none  [the longest x1 8.43 us: per_device(): jnp.dot(d_kv, w_shared_kv.T, preferred_element_type=jnp.float32)]
    unnamed x1 -> x0, blocking collectives: 67.1 us -> none
    convert_element_type x10 -> x0, other arithmetic: 27.4 us -> none  [the longest x1 18.3 us: per_device(): (d_h1 + norm_backward(d_n1, norm1_gain, normed1, factor1)).astype(jnp.bfl...]
    unnamed x114 -> x10, local copies, waits for them, and re-layouts: 28 us -> 6.74 us
  transfers between devices with their start and end apart: 9 -> 0, of which waited for: 9 -> 0; matrix products, arithmetic and copies ran while one was open for 6% -> 0% of each run, Pallas kernels for 0% -> 0%
where the time goes in v2:
time: 222 us
  Pallas kernels  213 us (96%)
  local copies, waits for them, and re-layouts  8.04 us (4%)
    pallas_call x1, Pallas kernels, per_device(): pl.pallas_call(block, out_shape=[jax.ShapeDtypeStruct(s, d) for s, d in o...  208 us
    unnamed x10, local copies, waits for them, and re-layouts  6.74 us
    pallas_call x1, Pallas kernels, per_device(): pl.pallas_call(finish, out_shape=[jax.ShapeDtypeStruct(s, d) for s, d in...  4.71 us

profile of v2, /device:TPU:1, one launch (start us, length us, event | category | flops | bytes accessed | tf_op | source)
XLA Modules:
  0.0 221.9 jit_solution(8261572036112783954)
XLA Ops:
  0.6 208.4 %shard_map.212 = (bf16[8,128,2048]{2,1,0:T(8,128)(2,1)}, bf16[8,128,2048]{2,1,0:T(8,128)(2,1)}, bf16[1024,256]{1,0:T(8,128)(2,1)}, f32[2624,128]{1,0:T(8,128)}, ...) custom-call(bf16[8,128,2048]{2,1,0:T(8,128)(2,1)} %bitcast.13, ...), custom_call_target="tpu_custom_call" | custom-call | tf_op jit(solution)/shard_map/pallas_call | solution.py:896
  209.1 0.0 copy-start
  209.1 2.2 copy-done
  211.3 0.0 copy-start.1
  211.3 2.2 copy-done.1
  213.4 0.0 copy-start.2
  213.4 1.3 copy-done.2
  214.8 0.0 copy-start.3
  214.8 1.0 copy-done.3
  215.8 0.0 copy-start.4
  215.8 4.7 %shard_map.213 = (bf16[1024,2048]{1,0:T(8,128)(2,1)}, bf16[1024,2048]{1,0:T(8,128)(2,1)}, bf16[1024,256]{1,0:T(8,128)(2,1)}, f32[128,256]{1,0:T(8,128)}, f32[256...) custom-call(bf16[1024,2048]{1,0:T(8,128)(2,1)S(1)} %bitcast.11, ...), custom_call_target="tpu_custom_call" | custom-call | tf_op jit(solution)/shard_map/pallas_call | solution.py:911
  220.5 0.0 copy-done.4
  220.5 0.7 slice_reduce_fusion
  221.2 0.6 slice.10
Async XLA Ops:
  209.1 2.2 copy-start
  211.3 2.2 copy-start.1
  213.4 1.3 copy-start.2
  214.8 1.0 copy-start.3
  215.8 4.7 %copy-start.4 = (f32[16,384]{1,0:T(8,128)S(1)}, f32[16,384]{1,0:T(8,128)}, u32[]{:S(2)}) copy-start(f32[16,384]{1,0:T(8,128)} %get-tuple-element.31) | copy-start | bytes 73732

commit v3 on v2

--- a/solution.py
+++ b/solution.py
@@ -62,6 +62,9 @@
         for dev in devs:
             pl.semaphore_signal(b, inc=1, device_id=dev, device_id_type=MESH)
         pl.semaphore_wait(b, len(devs))
+
+    def signal(self, sem, dev):
+        pl.semaphore_signal(sem, inc=1, device_id=dev, device_id_type=MESH)
 
     def take(self, n=1):
         at = self.used
@@ -322,7 +325,7 @@
     "kvo", "gsum", "kvsum", "n1h", "ph", "XB", "N2", "OC", "PA", "PB", "RC", "hp", "hm", "fp", "fm",
     "hp2", "hm2", "fp2", "fm2", "h1", "dh1", "xs", "stage2", "wqkv", "wov", "q", "kv",
     "att", "dq", "dkv", "csv", "hid", "dg", "du", "gn", "kvb", "kvr", "kvi", "dkvs",
-    "kvrc", "kvz", "kvx", "kvy", "kvct_v", "free_a", "free_b", "free_rc", "lsem", "send", "recv",
+    "kvrc", "kvz", "kvs", "dkw", "kvx", "kvy", "kvct_v", "gst", "free_a", "free_b", "free_rc", "free_rn", "lsem", "send", "recv",
 )
 
 
@@ -358,34 +361,40 @@
             bb = jnp.where(later, b[doc], bb)
         table = csv[s, 0:128]
         both = table * aa + pltpu.roll(table, 64, axis=1) * bb
-        other = pltpu.roll(both, 64, axis=1)
-        csv[s, 0:128] = jnp.where(low, both, other)
-        csv[s, 128:256] = jnp.where(low, -other, both)
-        csv[s, 256:384] = here.astype(F32)
+        csv[s, 0:128] = both
+        csv[s, 128:256] = here.astype(F32)
 
     loop(4, body)
 
 
-def finish(out, ig, kvo, gsum, out_f, ig_f, kv_f, gq, go, gg, gu, gd, query, sem):
-    copies = []
-
-    def copy(src, dst):
-        copies.append(pltpu.make_async_copy(src, dst, sem.at[len(copies)]))
-        copies[-1].start()
-
-    copy(gsum.at[pl.ds(2368, 256)], query)
+def cos_sin(csv, s):
+    both = csv[s, 0:128]
+    other = pltpu.roll(both, 64, axis=1)
+    low = lax.broadcasted_iota(jnp.int32, both.shape, 1) < 64
+    return jnp.where(low, both, other), jnp.where(low, -other, both)
+
+
+def finish(out, ig, kvo, gsum, out_f, ig_f, kv_f, gq, go, gg, gu, gd, big, mid, small, sem):
+    plan = []
     for i in range(4):
         s = pl.ds(256 * i, 256)
-        copy(out.at[s], out_f.at[s])
-        copy(ig.at[s], ig_f.at[s])
-    copy(kvo, kv_f)
-    copy(gsum.at[pl.ds(2112, 256)], go)
-    copy(gsum.at[pl.ds(704, 704)], gg)
-    copy(gsum.at[pl.ds(1408, 704)], gu)
-    copy(gsum.at[pl.ds(0, 704)], gd)
-    copies[0].wait()
-    gq[...] = query[...].T
-    for item in copies[1:]:
+        plan.append((out.at[s], big.at[i], out_f.at[s]))
+        plan.append((ig.at[s], big.at[4 + i], ig_f.at[s]))
+    plan.append((kvo, mid, kv_f))
+    for at, size, to in ((2112, 256, go), (704, 704, gg), (1408, 704, gu), (0, 704, gd)):
+        plan.append((gsum.at[pl.ds(at, size)], small.at[pl.ds(at, size)], to))
+    loads = [pltpu.make_async_copy(src, via, sem.at[0, n]) for n, (src, via, _) in enumerate(plan)]
+    loads.append(pltpu.make_async_copy(gsum.at[pl.ds(2368, 256)], small.at[pl.ds(2368, 256)], sem.at[0, len(plan)]))
+    for item in loads:
+        item.start()
+    stores = []
+    for n, (_, via, dst) in enumerate(plan):
+        loads[n].wait()
+        stores.append(pltpu.make_async_copy(via, dst, sem.at[1, n]))
+        stores[-1].start()
+    loads[-1].wait()
+    gq[...] = small[2368:2624].T
+    for item in stores:
         item.wait()
 
 
@@ -434,7 +443,7 @@
     def project(i):
         s = rows(i, 256)
         pre = dot(XB[pl.ds(2 * i, 2)].reshape(256, 2048), R.wqkv[...])
-        cos, sin = R.csv[s, 0:128], R.csv[s, 128:256]
+        cos, sin = cos_sin(R.csv, s)
         for h in range(2):
             R.q[s, 128 * h:128 * h + 128] = turn(pre[:, 128 * h:128 * h + 128], cos, sin).astype(BF16)
         R.kv[s, 0:128] = turn(pre[:, 256:384], cos, sin).astype(BF16)
@@ -456,7 +465,7 @@
         kk, vv = R.kv[ks, 0:128], R.kv[ks, 128:256]
         col = lax.broadcasted_iota(jnp.int32, (256, 768), 1) + ks.start
         row = lax.broadcasted_iota(jnp.int32, (256, 768), 0) + s.start
-        first = R.csv[s, 256:384][:, 0:1].astype(jnp.int32)
+        first = R.csv[s, 128:256][:, 0:1].astype(jnp.int32)
         bias = jnp.where((col <= row) & (col >= first), 0.0, NEGATIVE)
         done = []
         for h in range(2):
@@ -524,29 +533,31 @@
         st_n1.wait()
         st_p.wait()
 
-        def chunk(i):
-            d = i + i // 2 - 2 * (i // 3)
+        def out_part(j):
+            PB[pl.ds(2 * j, 2)] = dot(R.hid[rows(j, 256)], wdv[...]).astype(BF16).reshape(2, 128, 2048)
+
+        def chunk(d):
             j = (k.z + d) % 4
             s = rows(j, 256)
 
-            @pl.when(i == 0)
+            @pl.when(d == 0)
             def _():
                 g2.ready(0)
 
-            @pl.when(i == 1)
+            @pl.when(d == 1)
             def _():
                 g2.forward()
                 g2.share_near()
                 g2.ready(1)
 
-            @pl.when(i == 2)
-            def _():
-                g2.ready(3)
-
-            @pl.when(i == 3)
+            @pl.when(d == 2)
             def _():
                 g2.share_far()
                 g2.ready(2)
+
+            @pl.when(d == 3)
+            def _():
+                g2.ready(3)
 
             n2 = N2[pl.ds(2 * j, 2)].reshape(256, 2048)
             gate = dot(n2, wgv[...], NT)
@@ -560,6 +571,11 @@
             R.dg[s] = dg
             R.du[s] = du
 
+            @pl.when(d == 3)
+            def _():
+                dn.core_add(2)
+                dn.send("h1", "h2")
+
             def cols(n):
                 w = rows(n, 512)
                 part = dot(R.dg[s], wgv[:, w]) + dot(R.du[s], wuv[:, w])
@@ -568,29 +584,26 @@
             loop(4, cols)
             dn.swap(d)
 
-            @pl.when(i == 1)
+            @pl.when(d < 2)
+            def _():
+                out_part(j)
+
+            @pl.when(d == 1)
             def _():
                 dn.core_add(0)
 
-            @pl.when(i == 2)
+            @pl.when(d == 2)
             def _():
                 dn.core_add(1)
                 dn.send("u1")
 
-            @pl.when(i == 3)
-            def _():
-                dn.core_add(3)
-                dn.send("u2")
-
         loop(4, chunk)
 
-        dn.core_add(2)
-        dn.send("h1", "h2")
-
-        def out_part(i):
-            PB[pl.ds(2 * i, 2)] = dot(R.hid[rows(i, 256)], wdv[...]).astype(BF16).reshape(2, 128, 2048)
-
-        loop(4, out_part)
+        out_part((k.z + 2) % 4)
+        dn.core_add(3)
+        dn.send("u2")
+        k.signal(R.free_rc, k.sib())
+        out_part((k.z + 3) % 4)
 
     pl.run_scoped(
         mlp, b16(704, 2048), b16(704, 2048), b16(704, 2048),
@@ -598,6 +611,9 @@
     )
     g2.drain()
     dn.mid()
+    pl.semaphore_wait(R.free_rc, 1)
+    for d in range(4):
+        ou.swap(d)
 
     def weights(gm):
         sent_a, sent_b, sent_c, sent_d = [], [], [], []
@@ -612,9 +628,15 @@
 
             loop(8, body)
 
+        kept = {}
+
         def keep(offset):
             def store(at, count, value):
-                R.gsum[offset + at:offset + at + count] = value
+                slot = min(at, 1)
+                if slot in kept:
+                    kept[slot].wait()
+                R.gst[slot, 0:count] = value
+                kept[slot] = local(R.gst.at[slot, pl.ds(0, count)], R.gsum.at[pl.ds(offset + at, count)])
 
             return store
 
@@ -622,6 +644,10 @@
         xy_down = grads_xy(k, gm.at[0], bufs_a, keep(0), sent_a)
         next(xy_down, None)
         ld_p = local(R.ph, OC.at[:, :, pl.ds(0, 1536)])
+        for d in range(4):
+            ou.core_add(d)
+        ou.send("h1", "h2", "u1", "u2")
+        k.signal(R.free_rn, k.sib())
         dn.finish()
         R.gn[...] = jnp.zeros_like(R.gn)
 
@@ -642,44 +668,18 @@
         xy_gate = grads_xy(k, gm.at[1], bufs_b, keep(704), sent_b)
         next(xy_gate, None)
         next(xy_down, None)
-        gd.ready(0)
-        for d in range(4):
-            ou.swap(d)
+        ou.mid()
         gd.forward()
         grad(R.du, 0, 704, gm.at[2], 0, N2)
-        for d in range(4):
-            ou.core_add(d)
-        ou.send("h1", "h2", "u1", "u2")
-        pl.semaphore_signal(R.free_rc, inc=1, device_id=k.sib(), device_id_type=MESH)
-        gd.share_near()
-        next(xy_down, None)
-        next(xy_gate, None)
-        ld_p.wait()
+        R.dkv[...] = jnp.zeros_like(R.dkv)
         rn = ReduceZ(k, PA, R.RC, R.hp, R.hm, R.fp, R.fm)
-        pl.semaphore_wait(R.free_rc, 1)
-        R.dkv[...] = jnp.zeros_like(R.dkv)
-
-        def back(i):
-            d = i + i // 2 - 2 * (i // 3)
+
+        def back(d, between=None):
             j = (k.z + d) % 4
             s, ks = rows(j, 256), back_rows(j)
-
-            @pl.when(i == 1)
-            def _():
-                gd.ready(1)
-
-            @pl.when(i == 2)
-            def _():
-                gd.ready(3)
-
-            @pl.when(i == 3)
-            def _():
-                gd.share_far()
-                gd.ready(2)
-
             da = dot(XB[pl.ds(2 * j, 2)].reshape(256, 2048), R.wov[...], NT).astype(BF16)
             kk, vv = R.kv[ks, 0:128], R.kv[ks, 128:256]
-            cos, sin = R.csv[s, 0:128], R.csv[s, 128:256]
+            cos, sin = cos_sin(R.csv, s)
             done = []
             for h in range(2):
                 lanes = slice(128 * h, 128 * h + 128)
@@ -692,39 +692,57 @@
                 R.dkv[ks, 128:256] += dot(probs, da[:, lanes], TN)
             dq = jnp.concatenate(done, axis=1)
             R.dq[s] = dq
+            if between:
+                between()
             PA[pl.ds(2 * j, 2)] = dot(dq, R.wqkv[:, 0:256], NT).astype(BF16).reshape(2, 128, 2048)
             rn.swap(d)
 
-            @pl.when(i == 1)
-            def _():
-                rn.core_add(0)
-
-            @pl.when(i == 2)
-            def _():
-                rn.core_add(1)
-                rn.send("u1")
-
-            @pl.when(i == 3)
-            def _():
-                rn.core_add(3)
-                rn.send("u2")
-
-        loop(4, back)
-        rn.core_add(2)
-        rn.send("h1", "h2")
+        def shard4(i):
+            s = rows(i, 32)
+            R.stage2[s] = (R.h1[s] + ou.own(s)).astype(BF16)
+
+        gd.ready(0)
+        ld_p.wait()
+        pl.semaphore_wait(R.free_rn, 1)
+        back(0)
+        gd.share_near()
+        gd.ready(1)
+        back(1)
+        rn.core_add(0)
+        next(xy_down, None)
+        next(xy_gate, None)
+        ou.finish()
+        loop(4, shard4)
+        go = GatherZ(k, R.out, R.stage2)
+        go.start()
+        st_out = local(R.stage2, R.out.at[k.t])
+        gd.share_far()
+        gd.ready(2)
+        back(2)
+        rn.core_add(1)
+        rn.send("u1")
+        gd.ready(3)
+
+        def far():
+            rn.core_add(2)
+            rn.send("h1", "h2")
+
+        back(3, far)
         for d in range(4):
             for c in range(2):
                 R.kvb[c, d] = R.dkv[(2 * d + c) * 128:(2 * d + c) * 128 + 128].astype(BF16)
         kv_swap = k.go(R.kvb.at[1 - k.c], R.kvr, k.sib())
         ld_n1 = local(R.n1h, OC)
-        ou.mid()
+        rn.core_add(3)
+        rn.send("u2")
+        go.forward()
         for _ in xy_down:
             pass
         next(xy_gate, None)
 
         def hand_over(sent, free):
             for dev in (k.xdev(1), k.xdev(-1), k.ydev(1), k.ydev(-1)):
-                pl.semaphore_signal(free, inc=1, device_id=dev, device_id_type=MESH)
+                k.signal(free, dev)
             for copy in sent:
                 copy.wait_send()
             pl.semaphore_wait(free, 4)
@@ -736,10 +754,12 @@
         kv_swap.wait_recv()
         R.kvb[k.c] = R.kvb[k.c] + R.kvr[...]
         kv_in = [k.go(R.kvb.at[k.c, (k.z + d) % 4], R.kvi.at[d - 1], k.zdev(d)) for d in (1, 2, 3)]
+        go.share_near()
         gat = gm.at[0, :, :, pl.ds(0, 512)]
         grad(R.att, 0, 256, gat, 0, XB)
         next(xy_gate, None)
         next(xy_up, None)
+        go.share_far()
         ld_n1.wait()
         grad(R.dq, 0, 256, gat, 256, OC)
         for _ in xy_gate:
@@ -761,9 +781,12 @@
         for d in range(3):
             total = total + R.kvi[d].astype(F32)
         own = rows(k.t, 128)
-        cos, sin = R.csv[own, 0:128], R.csv[own, 128:256]
+        cos, sin = cos_sin(R.csv, own)
         R.dkvs[:, 0:128] = turn(total[:, 0:128], cos, -sin).astype(BF16)
         R.dkvs[:, 128:256] = total[:, 128:256].astype(BF16)
+        R.dkw[k.t] = R.dkvs[...]
+        dk_in = [k.go(R.dkvs, R.dkw.at[k.t], k.zdev(d)) for d in (1, 2, 3)]
+        dk_sib = [k.go(R.dkvs, R.dkw.at[k.t], k.sib())]
         rn.finish()
         gi = GatherZ(k, R.ig, R.xs)
 
@@ -772,57 +795,58 @@
             d = rn.own(s) + dot(R.dkvs[s], R.wqkv[:, 256:512], NT)
             y1, r1 = unit(R.xs[s].astype(F32))
             R.xs[s] = (R.dh1[s] + norm_back(d, R.gain1[...], y1, r1)).astype(BF16)
-            XB[k.t, s] = (y1 * R.gain1[...]).astype(BF16)
             dy = d * y1
             R.gn[1] += dy[0:8] + dy[8:16] + dy[16:24] + dy[24:32]
 
-        gd.drain()
-        R.gn[1] = jnp.zeros((8, 2048), F32)
         loop(4, shard3)
         gi.start()
         st_ig = local(R.xs, R.ig.at[k.t])
-        ou.finish()
-
-        def shard4(i):
-            s = rows(i, 32)
-            R.stage2[s] = (R.h1[s] + ou.own(s)).astype(BF16)
-
-        loop(4, shard4)
-        go = GatherZ(k, R.out, R.stage2)
-        go.start()
-        st_out = local(R.stage2, R.out.at[k.t])
-        small = dot(XB[k.t], R.dkvs[...], TN)
+        sm = gm.at[1]
         tops = [jnp.broadcast_to(jnp.sum(R.gn[i], axis=0, keepdims=True), (64, 2048)) for i in (1, 0)]
-        small = jnp.concatenate([small, jnp.concatenate(tops, axis=0).T], axis=1).astype(BF16)
-        sm = gm.at[1]
+        small = jnp.concatenate(tops, axis=0).T.astype(BF16)
         for e in range(128):
-            dp, at = e // 8, 48 * ((e % 2) * 4 + (e % 8) // 2)
-            for n in range(3):
-                sm[dp // 4, dp % 4, at + 16 * n:at + 16 * n + 16] = small[16 * e:16 * e + 16, 128 * n:128 * n + 128]
-        sm_swap = k.go(sm.at[:, :, pl.ds(192 * (1 - k.c), 192)], R.kvrc, k.sib())
+            dp, at = e // 8, 256 + 16 * ((e % 2) * 4 + (e % 8) // 2)
+            sm[dp // 4, dp % 4, at:at + 16] = small[16 * e:16 * e + 16]
+        sm_swap = k.go(sm.at[:, :, pl.ds(256 + 64 * (1 - k.c), 64)], R.kvrc, k.sib())
+        for copy in dk_in:
+            copy.wait_recv()
+        dk_sib += [k.go(R.dkw.at[k.slot(d)], R.dkw.at[k.slot(d)], k.sib()) for d in (1, 2, 3)]
+        next(xy_att, None)
+        next(xy_up, None)
+        for copy in dk_sib:
+            copy.wait_recv()
+        dkw = R.dkw[...].reshape(1024, 256)
+
+        def grad_kv(n):
+            res = dot(OC[:, :, rows(n, 256)].reshape(1024, 256), dkw, TN).astype(BF16)
+            for e in range(16):
+                dp = 2 * n + e // 8
+                for half in range(2):
+                    at = 32 * (e % 8) + 16 * half
+                    sm[dp // 4, dp % 4, at:at + 16] = res[16 * e:16 * e + 16, 128 * half:128 * half + 128]
+
+        loop(8, grad_kv)
+        sm_swap.wait_recv()
+        for e in range(16):
+            at = sm.at[e // 4, e % 4, pl.ds(256 + 64 * k.c, 64)]
+            at[...] = at[...] + R.kvrc[e // 4, e % 4]
+        mine = lambda d: sm.at[:, :, pl.ds(256 + 64 * k.c + 16 * ((k.z + d) % 4), 16)]
+        z_in = [k.go(mine(d), R.kvz.at[d - 1], k.zdev(d)) for d in (1, 2, 3)]
         next(xy_att, None)
         next(xy_up, None)
         gi.forward()
-        sm_swap.wait_recv()
-        for e in range(16):
-            at = sm.at[e // 4, e % 4, pl.ds(192 * k.c, 192)]
-            at[...] = at[...] + R.kvrc[e // 4, e % 4]
-        mine = lambda d: sm.at[:, :, pl.ds(192 * k.c + 48 * ((k.z + d) % 4), 48)]
-        z_in = [k.go(mine(d), R.kvz.at[d - 1], k.zdev(d)) for d in (1, 2, 3)]
-        next(xy_att, None)
-        next(xy_up, None)
         for copy in z_in:
             copy.wait_recv()
-        R.kvz[3] = (mine(0)[...].astype(F32) + sum(R.kvz[i].astype(F32) for i in range(3))).astype(BF16)
-        x_in = [k.go(R.kvz.at[3, (k.x + d) % 4], R.kvx.at[d - 1], k.xdev(d)) for d in (1, 2, 3)]
+        for e in range(16):
+            q = (e // 4, e % 4)
+            R.kvs[q[0], q[1], 0:32] = sm[q[0], q[1], pl.ds(32 * k.t, 32)]
+            own = sm[q[0], q[1], pl.ds(256 + 64 * k.c + 16 * k.z, 16)].astype(F32)
+            R.kvs[q[0], q[1], 32:48] = (own + sum(R.kvz[i, q[0], q[1]].astype(F32) for i in range(3))).astype(BF16)
+        x_in = [k.go(R.kvs.at[(k.x + d) % 4], R.kvx.at[d - 1], k.xdev(d)) for d in (1, 2, 3)]
         gi.share_near()
-        go.forward()
-        go.share_near()
         for copy in x_in:
             copy.wait_recv()
-        R.kvx[3] = (
-            R.kvz[3, k.x].astype(F32) + sum(R.kvx[i].astype(F32) for i in range(3))
-        ).astype(BF16)
+        R.kvx[3] = (R.kvs[k.x].astype(F32) + sum(R.kvx[i].astype(F32) for i in range(3))).astype(BF16)
         y_in = [k.go(R.kvx.at[3, (k.y + d) % 4], R.kvy.at[d - 1], k.ydev(d)) for d in (1, 2, 3)]
         next(xy_att, None)
         next(xy_up, None)
@@ -831,20 +855,19 @@
         whole = R.kvx[3, k.y].astype(F32) + sum(R.kvy[i].astype(F32) for i in range(3))
         for n in range(3):
             R.kvsum[:, 128 * n:128 * n + 128] = whole[16 * n:16 * n + 16]
-        gi.share_far()
         for xy in (xy_att, xy_up):
             for _ in xy:
                 pass
-        go.share_far()
-        for ag in (gi, go):
+        gi.share_far()
+        for ag in (go, gi):
             for d in (0, 1, 3, 2):
                 ag.ready(d)
-        for copy in sent_c + sent_d + kv_in + z_in + x_in + y_in + [kv_swap, sm_swap]:
+        for copy in sent_c + sent_d + kv_in + dk_in + dk_sib + z_in + x_in + y_in + [kv_swap, sm_swap]:
             copy.wait_send()
-        for item in (rn, ou, gi, go):
+        for item in (gd, rn, ou, gi, go):
             item.drain()
-        st_ig.wait()
-        st_out.wait()
+        for copy in (st_ig, st_out, kept[0], kept[1]):
+            copy.wait()
 
     R.stage2[...] = OC[k.t]
     pl.run_scoped(weights, pltpu.VMEM((3, 4, 4, 704, 128), BF16))
@@ -886,10 +909,10 @@
         [big] * 5 + [core] + hops + hops
         + [b32(128, 2048), b32(128, 2048), b16(128, 2048), b16(128, 2048)]
         + [b16(2048, 512), b16(256, 2048), b16(1024, 256), b16(1024, 256), b16(1024, 256), b16(1024, 256)]
-        + [b32(1024, 256), b32(1024, 384), b16(1024, 704), b16(1024, 704), b16(1024, 704), b32(2, 8, 2048)]
+        + [b32(1024, 256), b32(1024, 256), b16(1024, 704), b16(1024, 704), b16(1024, 704), b32(2, 8, 2048)]
         + [b16(2, 4, 128, 256), b16(4, 128, 256), b16(3, 128, 256), b16(128, 256)]
-        + [b16(4, 4, 192, 128), b16(4, 4, 4, 48, 128), b16(4, 4, 48, 128), b16(3, 48, 128)]
-        + [b32(128, 256), pltpu.SemaphoreType.REGULAR] + [pltpu.SemaphoreType.REGULAR] * 2 + [pltpu.SemaphoreType.DMA((16,))]
+        + [b16(4, 4, 64, 128), b16(3, 4, 4, 16, 128), b16(4, 4, 48, 128), b16(8, 128, 256), b16(4, 4, 48, 128), b16(3, 48, 128)]
+        + [b32(128, 256), b32(2, 352, 128), pltpu.SemaphoreType.REGULAR] + [pltpu.SemaphoreType.REGULAR] * 3 + [pltpu.SemaphoreType.DMA((24,))]
         + [pltpu.SemaphoreType.DMA((NSEM,)), pltpu.SemaphoreType.DMA((NSEM,))]
         + grads_bufs(704) + grads_bufs(704)
     )
@@ -897,7 +920,7 @@
         block,
         out_shape=[jax.ShapeDtypeStruct(s, d) for s, d in outs],
         in_specs=[ANY] * 10 + [VM] * 2 + [pl.BlockSpec(memory_space=pltpu.SMEM)],
-        out_specs=[ANY] * 3 + [VM] * 2 + [ANY] * 2,
+        out_specs=[ANY] * 4 + [VM] + [ANY] * 2,
         scratch_shapes=scratch,
         compiler_params=pltpu.CompilerParams(
             collective_id=0, has_side_effects=True, vmem_limit_bytes=VLIM
@@ -913,8 +936,8 @@
         out_shape=[jax.ShapeDtypeStruct(s, d) for s, d in shapes],
         in_specs=[ANY] * 4,
         out_specs=[ANY] * 3 + [VM] + [ANY] * 4,
-        scratch_shapes=[b32(256, 128), pltpu.SemaphoreType.DMA((14,))],
-        compiler_params=pltpu.CompilerParams(vmem_limit_bytes=8 * 2**20),
+        scratch_shapes=[b16(8, 256, 2048), b16(1024, 256), b32(2624, 128), pltpu.SemaphoreType.DMA((2, 14))],
+        compiler_params=pltpu.CompilerParams(vmem_limit_bytes=VLIM),
     )(flat(output), flat(input_grad), shared_kv, gsum)
     return (
         output, input_grad, shared_kv, kvsum[:, 256], g_query, kvsum[:, 0:256], g_out, kvsum[:, 320],
@@ -922,7 +945,7 @@
     )
 
 
-VLIM = 63 * 2**20
+VLIM = 63 * 2**20 + 2**19
 
 
 def solution(mesh):

time: 222 us -> 205 us (0.923)
  Pallas kernels: 213 us -> 203 us
  local copies, waits for them, and re-layouts: 8.04 us -> 1.31 us
    pallas_call x1, Pallas kernels: 208 us -> 194 us  [per_device(): pl.pallas_call(block, out_shape=[jax.ShapeDtypeStruct(s, d) for s, d in o...]
    unnamed x10 -> x2, local copies, waits for them, and re-layouts: 6.74 us -> 0.01 us
    pallas_call x1, Pallas kernels: 4.71 us -> 8.27 us  [per_device(): pl.pallas_call(finish, out_shape=[jax.ShapeDtypeStruct(s, d) for s, d in...]
where the time goes in v3:
time: 205 us
  Pallas kernels  203 us (99%)
    pallas_call x1, Pallas kernels, per_device(): pl.pallas_call(block, out_shape=[jax.ShapeDtypeStruct(s, d) for s, d in o...  194 us
    pallas_call x1, Pallas kernels, per_device(): pl.pallas_call(finish, out_shape=[jax.ShapeDtypeStruct(s, d) for s, d in...  8.27 us

profile of v3, /device:TPU:1, one launch (start us, length us, event | category | flops | bytes accessed | tf_op | source)
XLA Modules:
  0.0 204.7 jit_solution(3362166882579583814)
XLA Ops:
  0.6 194.5 %shard_map.212 = (bf16[8,128,2048]{2,1,0:T(8,128)(2,1)}, bf16[8,128,2048]{2,1,0:T(8,128)(2,1)}, bf16[1024,256]{1,0:T(8,128)(2,1)}, f32[2624,128]{1,0:T(8,128)}, ...) custom-call(bf16[8,128,2048]{2,1,0:T(8,128)(2,1)} %bitcast.13, ...), custom_call_target="tpu_custom_call" | custom-call | tf_op jit(solution)/shard_map/pallas_call | solution.py:919
  195.1 0.0 copy-start
  195.1 8.3 %shard_map.213 = (bf16[1024,2048]{1,0:T(8,128)(2,1)}, bf16[1024,2048]{1,0:T(8,128)(2,1)}, bf16[1024,256]{1,0:T(8,128)(2,1)}, f32[128,256]{1,0:T(8,128)}, f32[256...) custom-call(bf16[1024,2048]{1,0:T(8,128)(2,1)} %bitcast.11, ...), custom_call_target="tpu_custom_call" | custom-call | tf_op jit(solution)/shard_map/pallas_call | solution.py:934
  203.4 0.0 copy-done
  203.4 0.7 slice_reduce_fusion
  204.1 0.6 slice.10
Async XLA Ops:
  195.1 8.3 %copy-start = (f32[16,384]{1,0:T(8,128)S(1)}, f32[16,384]{1,0:T(8,128)}, u32[]{:S(2)}) copy-start(f32[16,384]{1,0:T(8,128)} %get-tuple-element.31) | copy-start | bytes 73732

commit v4 on v3

--- a/solution.py
+++ b/solution.py
@@ -57,11 +57,11 @@
     def ydev(self, d):
         return (self.x * 4 + (self.y + d) % 4, self.t)
 
-    def barrier(self, devs):
+    def greet(self, devs):
         b = pltpu.get_barrier_semaphore()
         for dev in devs:
             pl.semaphore_signal(b, inc=1, device_id=dev, device_id_type=MESH)
-        pl.semaphore_wait(b, len(devs))
+        return lambda: pl.semaphore_wait(b, len(devs))
 
     def signal(self, sem, dev):
         pl.semaphore_signal(sem, inc=1, device_id=dev, device_id_type=MESH)
@@ -92,24 +92,24 @@
 
 class ReduceZ:
     def __init__(self, k, part, rc, hp, hm, fp, fm):
-        self.k, self.part, self.rc = k, part, rc
+        self.k, self.part, (self.rc_to, self.rc_of) = k, part, rc
         self.hp, self.hm, self.fp, self.fm = hp, hm, fp, fm
         self.base = k.take(10)
 
     def _swap(self, d):
         k = self.k
-        return k.copy(self.base + d, self.part.at[k.slot(d, 1 - k.c)], self.rc.at[d], k.sib())
+        return k.copy(self.base + d, self.part.at[k.slot(d, 1 - k.c)], self.rc_to(d), k.sib())
 
     def swap(self, d):
         self._swap(d).start()
 
     def core_add(self, d):
         self._swap(d).wait_recv()
-        mine = self.part.at[self.k.slot(d)]
+        mine, theirs = self.part.at[self.k.slot(d)], self.rc_of(d)
 
         def body(i):
             s = rows(i, 32)
-            mine[s] = mine[s] + self.rc[d, s]
+            mine[s] = mine[s] + theirs[s]
 
         loop(4, body)
 
@@ -322,10 +322,10 @@
 NSEM = 256
 NAMES = (
     "x", "oc", "wq", "wkv", "wo", "wg", "wu", "wd", "kvct", "cs", "gain1", "gain2", "lens", "out", "ig",
-    "kvo", "gsum", "kvsum", "n1h", "ph", "XB", "N2", "OC", "PA", "PB", "RC", "hp", "hm", "fp", "fm",
+    "kvo", "gsum", "kvsum", "n1h", "ph", "wall", "XB", "N2", "OC", "PA", "PB", "RC", "hp", "hm", "fp", "fm",
     "hp2", "hm2", "fp2", "fm2", "h1", "dh1", "xs", "stage2", "wqkv", "wov", "q", "kv",
     "att", "dq", "dkv", "csv", "hid", "dg", "du", "gn", "kvb", "kvr", "kvi", "dkvs",
-    "kvrc", "kvz", "kvs", "dkw", "kvx", "kvy", "kvct_v", "gst", "free_a", "free_b", "free_rc", "free_rn", "lsem", "send", "recv",
+    "dqw", "kvx", "kvy", "nvx", "nvs", "nvy", "nvt", "nvr", "kvct_v", "gst", "free_a", "free_b",  "lsem", "send", "recv",
 )
 
 
@@ -414,17 +414,25 @@
         copy.start()
         return copy
 
+    greeted = k.greet(
+        [k.zdev(1), k.zdev(-1), k.zdev(2), k.sib()]
+        + [(k.dp, k.slot(d, 1 - k.c)) for d in (1, 2, 3)]
+        + [dev(d) for dev in (k.xdev, k.ydev) for d in (1, 2, 3)]
+    )
+    ld_q = local(R.wq, R.wqkv.at[:, pl.ds(0, 256)])
     ld_x = local(R.x, XB)
-    ld_q = local(R.wq, R.wqkv.at[:, pl.ds(0, 256)])
     ld_kv = local(R.wkv, R.wqkv.at[:, pl.ds(256, 256)])
     ld_cs = local(R.cs, R.csv.at[:, pl.ds(0, 128)])
     ld_wo = local(R.wo, R.wov)
     ld_oc = local(R.oc, OC)
     ld_ct = local(R.kvct.at[k.t], R.kvct_v)
-    k.barrier(
-        [k.zdev(1), k.zdev(-1), k.zdev(2), k.sib()]
-        + [dev(d) for dev in (k.xdev, k.ydev) for d in (1, 2, 3)]
-    )
+    ld_q.wait()
+
+    def turn_wq(i):
+        s = rows(i, 256)
+        PB[0:2, :, s] = R.wqkv[s, 0:256].T.reshape(2, 128, 256)
+
+    loop(8, turn_wq)
 
     ld_x.wait()
     R.xs[...] = XB[k.t]
@@ -435,9 +443,15 @@
 
     loop(16, norm1)
     st_n1 = local(XB, R.n1h)
+    greeted()
+    W, half = R.wall, k.y // 2
+    slim = pl.ds(pl.multiple_of(64 * (k.y % 2) + 16 * k.x, 16), 16)
+    wide = pl.ds(pl.multiple_of(64 * (k.y % 2), 64), 64)
+    w_z = [k.go(PB.at[half, slim], W.at[d, k.c, half, slim], k.zdev(-d)) for d in (1, 2, 3)]
+    w_own = k.go(PB.at[pl.ds(0, 2)], W.at[0, k.c], k.sib())
+    st_w = local(PB.at[pl.ds(0, 2)], W.at[0, k.c])
     ld_cs.wait()
     rope_rows(R.lens, R.csv)
-    ld_q.wait()
     ld_kv.wait()
 
     def project(i):
@@ -456,7 +470,17 @@
     def back_rows(j):
         return pl.ds(pl.multiple_of((j // 2) * (j - 2) * 256, 256), 768)
 
-    rs = ReduceZ(k, PA, R.RC, R.hp, R.hm, R.fp, R.fm)
+    by_turn = (lambda d: R.RC.at[d],) * 2
+    by_slot = (lambda d: XB.at[k.slot(d, 1 - k.c)], lambda d: XB.at[k.slot(d)])
+    rs = ReduceZ(k, PA, by_turn, R.hp, R.hm, R.fp, R.fm)
+
+    for copy in w_z:
+        copy.wait_recv()
+    near = W.at[pl.ds(1, 3), k.c, half, slim]
+    w_x = [k.go(near, near, k.xdev(d)) for d in (1, 2, 3)]
+    for copy in w_z + [w_own]:
+        copy.wait_send()
+    st_w.wait()
 
     def attend(i):
         d = (2 - i + 3 * (i // 2) - 2 * (i // 3)) % 4
@@ -498,9 +522,13 @@
     st_p = local(PB.at[:, :, pl.ds(0, 1536)], R.ph)
     rs.core_add(0)
     rs.mid()
+    for copy in w_x:
+        copy.wait_recv()
+    near = W.at[pl.ds(1, 3), k.c, half, wide]
+    w_y = [k.go(near, near, k.ydev(d)) for d in (1, 2, 3)]
     g2 = GatherZ(k, N2, N2.at[k.t])
-    dn = ReduceZ(k, PA, R.RC, R.hp, R.hm, R.fp, R.fm)
-    ou = ReduceZ(k, PB, R.RC, R.hp2, R.hm2, R.fp2, R.fm2)
+    dn = ReduceZ(k, PA, by_turn, R.hp, R.hm, R.fp, R.fm)
+    ou = ReduceZ(k, PB, by_slot, R.hp2, R.hm2, R.fp2, R.fm2)
     gd = GatherZ(k, XB, XB.at[k.t])
 
     def mlp(wgv, wuv, wdv, wsem):
@@ -526,12 +554,12 @@
             N2[k.t, s] = (unit(h1)[0] * R.gain2[...]).astype(BF16)
 
         loop(4, shard1)
+        st_n1.wait()
+        st_p.wait()
         g2.start()
         rs.drain()
         lg.wait()
         lu.wait()
-        st_n1.wait()
-        st_p.wait()
 
         def out_part(j):
             PB[pl.ds(2 * j, 2)] = dot(R.hid[rows(j, 256)], wdv[...]).astype(BF16).reshape(2, 128, 2048)
@@ -584,9 +612,8 @@
             loop(4, cols)
             dn.swap(d)
 
-            @pl.when(d < 2)
-            def _():
-                out_part(j)
+            out_part(j)
+            ou.swap(d)
 
             @pl.when(d == 1)
             def _():
@@ -596,14 +623,20 @@
             def _():
                 dn.core_add(1)
                 dn.send("u1")
+                ou.core_add(0)
+                ou.core_add(1)
+                ou.send("u1")
+
+            @pl.when(d == 3)
+            def _():
+                ou.core_add(2)
+                ou.send("h1", "h2")
 
         loop(4, chunk)
-
-        out_part((k.z + 2) % 4)
         dn.core_add(3)
         dn.send("u2")
-        k.signal(R.free_rc, k.sib())
-        out_part((k.z + 3) % 4)
+        ou.core_add(3)
+        ou.send("u2")
 
     pl.run_scoped(
         mlp, b16(704, 2048), b16(704, 2048), b16(704, 2048),
@@ -611,9 +644,10 @@
     )
     g2.drain()
     dn.mid()
-    pl.semaphore_wait(R.free_rc, 1)
-    for d in range(4):
-        ou.swap(d)
+    for copy in w_y:
+        copy.wait_recv()
+    near = W.at[pl.ds(1, 3), k.c]
+    w_core = k.go(near, near, k.sib())
 
     def weights(gm):
         sent_a, sent_b, sent_c, sent_d = [], [], [], []
@@ -644,10 +678,7 @@
         xy_down = grads_xy(k, gm.at[0], bufs_a, keep(0), sent_a)
         next(xy_down, None)
         ld_p = local(R.ph, OC.at[:, :, pl.ds(0, 1536)])
-        for d in range(4):
-            ou.core_add(d)
-        ou.send("h1", "h2", "u1", "u2")
-        k.signal(R.free_rn, k.sib())
+        ou.mid()
         dn.finish()
         R.gn[...] = jnp.zeros_like(R.gn)
 
@@ -668,13 +699,36 @@
         xy_gate = grads_xy(k, gm.at[1], bufs_b, keep(704), sent_b)
         next(xy_gate, None)
         next(xy_down, None)
-        ou.mid()
+        ou.finish()
+
+        def shard4(i):
+            s = rows(i, 32)
+            R.stage2[s] = (R.h1[s] + ou.own(s)).astype(BF16)
+
+        loop(4, shard4)
+        go = GatherZ(k, R.out, R.stage2)
+        go.start()
+        st_out = local(R.stage2, R.out.at[k.t])
         gd.forward()
         grad(R.du, 0, 704, gm.at[2], 0, N2)
+        next(xy_down, None)
+        next(xy_gate, None)
+        w_own.wait_recv()
+        w_core.wait_recv()
+
+        def w_block(d, c):
+            i = 2 * d + c
+            return (PA if i < 4 else N2), pl.ds(2 * (i % 4), 2)
+
+        ld_w = []
+        for d in range(4):
+            for c in range(2):
+                buf, at = w_block(d, c)
+                ld_w.append(local(W.at[d, c], buf.at[at]))
         R.dkv[...] = jnp.zeros_like(R.dkv)
-        rn = ReduceZ(k, PA, R.RC, R.hp, R.hm, R.fp, R.fm)
-
-        def back(d, between=None):
+        dq_in = []
+
+        def back(d):
             j = (k.z + d) % 4
             s, ks = rows(j, 256), back_rows(j)
             da = dot(XB[pl.ds(2 * j, 2)].reshape(256, 2048), R.wov[...], NT).astype(BF16)
@@ -692,79 +746,54 @@
                 R.dkv[ks, 128:256] += dot(probs, da[:, lanes], TN)
             dq = jnp.concatenate(done, axis=1)
             R.dq[s] = dq
-            if between:
-                between()
-            PA[pl.ds(2 * j, 2)] = dot(dq, R.wqkv[:, 0:256], NT).astype(BF16).reshape(2, 128, 2048)
-            rn.swap(d)
-
-        def shard4(i):
-            s = rows(i, 32)
-            R.stage2[s] = (R.h1[s] + ou.own(s)).astype(BF16)
+            for c in (k.c, 1 - k.c) if d else (1 - k.c,):
+                to = k.slot(d, c)
+                dq_in.append(k.go(R.dq.at[rows(to, 128)], R.dqw.at[k.t], (k.dp, to)))
+
+        def give(free):
+            for dev in (k.xdev(1), k.xdev(-1), k.ydev(1), k.ydev(-1)):
+                k.signal(free, dev)
 
         gd.ready(0)
         ld_p.wait()
-        pl.semaphore_wait(R.free_rn, 1)
         back(0)
         gd.share_near()
         gd.ready(1)
-        back(1)
-        rn.core_add(0)
         next(xy_down, None)
         next(xy_gate, None)
-        ou.finish()
-        loop(4, shard4)
-        go = GatherZ(k, R.out, R.stage2)
-        go.start()
-        st_out = local(R.stage2, R.out.at[k.t])
+        back(1)
+        for _ in xy_down:
+            pass
+        give(R.free_a)
+        next(xy_gate, None)
+        go.forward()
         gd.share_far()
         gd.ready(2)
         back(2)
-        rn.core_add(1)
-        rn.send("u1")
+        pl.semaphore_wait(R.free_a, 4)
+        xy_up = grads_xy(k, gm.at[2], bufs_a, keep(1408), sent_c)
+        next(xy_up, None)
+        go.share_near()
         gd.ready(3)
-
-        def far():
-            rn.core_add(2)
-            rn.send("h1", "h2")
-
-        back(3, far)
+        back(3)
         for d in range(4):
             for c in range(2):
                 R.kvb[c, d] = R.dkv[(2 * d + c) * 128:(2 * d + c) * 128 + 128].astype(BF16)
         kv_swap = k.go(R.kvb.at[1 - k.c], R.kvr, k.sib())
         ld_n1 = local(R.n1h, OC)
-        rn.core_add(3)
-        rn.send("u2")
-        go.forward()
-        for _ in xy_down:
+        for _ in xy_gate:
             pass
-        next(xy_gate, None)
-
-        def hand_over(sent, free):
-            for dev in (k.xdev(1), k.xdev(-1), k.ydev(1), k.ydev(-1)):
-                k.signal(free, dev)
-            for copy in sent:
-                copy.wait_send()
-            pl.semaphore_wait(free, 4)
-
-        hand_over(sent_a, R.free_a)
-        xy_up = grads_xy(k, gm.at[2], bufs_a, keep(1408), sent_c)
-        next(xy_up, None)
-        rn.mid()
+        give(R.free_b)
+        for copy in sent_a + sent_b:
+            copy.wait_send()
+        gat = gm.at[0, :, :, pl.ds(0, 512)]
+        grad(R.att, 0, 256, gat, 0, XB)
         kv_swap.wait_recv()
         R.kvb[k.c] = R.kvb[k.c] + R.kvr[...]
         kv_in = [k.go(R.kvb.at[k.c, (k.z + d) % 4], R.kvi.at[d - 1], k.zdev(d)) for d in (1, 2, 3)]
-        go.share_near()
-        gat = gm.at[0, :, :, pl.ds(0, 512)]
-        grad(R.att, 0, 256, gat, 0, XB)
-        next(xy_gate, None)
-        next(xy_up, None)
-        go.share_far()
         ld_n1.wait()
         grad(R.dq, 0, 256, gat, 256, OC)
-        for _ in xy_gate:
-            pass
-        hand_over(sent_b, R.free_b)
+        pl.semaphore_wait(R.free_b, 4)
 
         def part(buf, n):
             return buf.at[:, pl.ds(0, n)] if len(buf.shape) == 3 else buf.at[pl.ds(0, n)]
@@ -774,6 +803,22 @@
         xy_att = grads_xy(k, gat, bufs_c, keep(2112), sent_d)
         next(xy_att, None)
         next(xy_up, None)
+        R.dqw[k.t] = R.dq[rows(k.t, 128)]
+        for copy in dq_in:
+            copy.wait_recv()
+        for copy in ld_w:
+            copy.wait()
+
+        def d_n1(n):
+            w = rows(n, 512)
+            total = jnp.zeros((128, 512), F32)
+            for d in range(4):
+                for c in range(2):
+                    buf, at = w_block(d, c)
+                    total = total + dot(R.dqw[k.slot(d, c)], buf[at, :, w].reshape(256, 512))
+            R.h1[:, w] = total
+
+        loop(4, d_n1)
         for copy in kv_in:
             copy.wait_recv()
         ld_ct.wait()
@@ -784,15 +829,15 @@
         cos, sin = cos_sin(R.csv, own)
         R.dkvs[:, 0:128] = turn(total[:, 0:128], cos, -sin).astype(BF16)
         R.dkvs[:, 128:256] = total[:, 128:256].astype(BF16)
-        R.dkw[k.t] = R.dkvs[...]
-        dk_in = [k.go(R.dkvs, R.dkw.at[k.t], k.zdev(d)) for d in (1, 2, 3)]
-        dk_sib = [k.go(R.dkvs, R.dkw.at[k.t], k.sib())]
-        rn.finish()
+        dkw = R.q
+        dkw[own] = R.dkvs[...]
+        dk_in = [k.go(R.dkvs, dkw.at[own], k.zdev(d)) for d in (1, 2, 3)]
+        dk_sib = [k.go(R.dkvs, dkw.at[own], k.sib())]
         gi = GatherZ(k, R.ig, R.xs)
 
         def shard3(i):
             s = rows(i, 32)
-            d = rn.own(s) + dot(R.dkvs[s], R.wqkv[:, 256:512], NT)
+            d = R.h1[s] + dot(R.dkvs[s], R.wqkv[:, 256:512], NT)
             y1, r1 = unit(R.xs[s].astype(F32))
             R.xs[s] = (R.dh1[s] + norm_back(d, R.gain1[...], y1, r1)).astype(BF16)
             dy = d * y1
@@ -802,23 +847,28 @@
         gi.start()
         st_ig = local(R.xs, R.ig.at[k.t])
         sm = gm.at[1]
-        tops = [jnp.broadcast_to(jnp.sum(R.gn[i], axis=0, keepdims=True), (64, 2048)) for i in (1, 0)]
-        small = jnp.concatenate(tops, axis=0).T.astype(BF16)
-        for e in range(128):
-            dp, at = e // 8, 256 + 16 * ((e % 2) * 4 + (e % 8) // 2)
-            sm[dp // 4, dp % 4, at:at + 16] = small[16 * e:16 * e + 16]
-        sm_swap = k.go(sm.at[:, :, pl.ds(256 + 64 * (1 - k.c), 64)], R.kvrc, k.sib())
+        two = [jnp.sum(R.gn[i], axis=0, keepdims=True) for i in (1, 0)]
+        two = jnp.concatenate(two + [jnp.zeros((14, 2048), F32)], axis=0).astype(BF16)
+        for e in range(16):
+            sm[e // 4, e % 4, 256:272] = two[:, 128 * e:128 * e + 128]
+        line = pl.ds(256, 16)
+        nx = [k.go(sm.at[(k.x + d) % 4, :, line], R.nvx.at[d - 1], k.xdev(d)) for d in (1, 2, 3)]
         for copy in dk_in:
             copy.wait_recv()
-        dk_sib += [k.go(R.dkw.at[k.slot(d)], R.dkw.at[k.slot(d)], k.sib()) for d in (1, 2, 3)]
+        theirs = [dkw.at[rows(k.slot(d), 128)] for d in (1, 2, 3)]
+        dk_sib += [k.go(piece, piece, k.sib()) for piece in theirs]
+        go.share_far()
         next(xy_att, None)
         next(xy_up, None)
+        for copy in nx:
+            copy.wait_recv()
+        R.nvs[...] = (sm[k.x, :, line].astype(F32) + sum(R.nvx[i].astype(F32) for i in range(3))).astype(BF16)
+        ny = [k.go(R.nvs.at[(k.y + d) % 4], R.nvy.at[d - 1], k.ydev(d)) for d in (1, 2, 3)]
         for copy in dk_sib:
             copy.wait_recv()
-        dkw = R.dkw[...].reshape(1024, 256)
 
         def grad_kv(n):
-            res = dot(OC[:, :, rows(n, 256)].reshape(1024, 256), dkw, TN).astype(BF16)
+            res = dot(OC[:, :, rows(n, 256)].reshape(1024, 256), dkw[...], TN).astype(BF16)
             for e in range(16):
                 dp = 2 * n + e // 8
                 for half in range(2):
@@ -826,35 +876,29 @@
                     sm[dp // 4, dp % 4, at:at + 16] = res[16 * e:16 * e + 16, 128 * half:128 * half + 128]
 
         loop(8, grad_kv)
-        sm_swap.wait_recv()
-        for e in range(16):
-            at = sm.at[e // 4, e % 4, pl.ds(256 + 64 * k.c, 64)]
-            at[...] = at[...] + R.kvrc[e // 4, e % 4]
-        mine = lambda d: sm.at[:, :, pl.ds(256 + 64 * k.c + 16 * ((k.z + d) % 4), 16)]
-        z_in = [k.go(mine(d), R.kvz.at[d - 1], k.zdev(d)) for d in (1, 2, 3)]
-        next(xy_att, None)
-        next(xy_up, None)
+        mine = pl.ds(pl.multiple_of(32 * k.t, 32), 32)
+        x_in = [k.go(sm.at[(k.x + d) % 4, :, mine], R.kvx.at[d - 1], k.xdev(d)) for d in (1, 2, 3)]
+        for copy in ny:
+            copy.wait_recv()
+        R.nvt[...] = (R.nvs[k.y].astype(F32) + sum(R.nvy[i].astype(F32) for i in range(3))).astype(BF16)
+        peers = [k.slot(d) for d in (1, 2, 3)] + [k.slot(d, 1 - k.c) for d in (0, 1, 2, 3)]
+        nt = [k.go(R.nvt, R.nvr.at[i], (k.dp, peer)) for i, peer in enumerate(peers)]
         gi.forward()
-        for copy in z_in:
-            copy.wait_recv()
-        for e in range(16):
-            q = (e // 4, e % 4)
-            R.kvs[q[0], q[1], 0:32] = sm[q[0], q[1], pl.ds(32 * k.t, 32)]
-            own = sm[q[0], q[1], pl.ds(256 + 64 * k.c + 16 * k.z, 16)].astype(F32)
-            R.kvs[q[0], q[1], 32:48] = (own + sum(R.kvz[i, q[0], q[1]].astype(F32) for i in range(3))).astype(BF16)
-        x_in = [k.go(R.kvs.at[(k.x + d) % 4], R.kvx.at[d - 1], k.xdev(d)) for d in (1, 2, 3)]
-        gi.share_near()
         for copy in x_in:
             copy.wait_recv()
-        R.kvx[3] = (R.kvs[k.x].astype(F32) + sum(R.kvx[i].astype(F32) for i in range(3))).astype(BF16)
+        R.kvx[3] = (sm[k.x, :, mine].astype(F32) + sum(R.kvx[i].astype(F32) for i in range(3))).astype(BF16)
         y_in = [k.go(R.kvx.at[3, (k.y + d) % 4], R.kvy.at[d - 1], k.ydev(d)) for d in (1, 2, 3)]
         next(xy_att, None)
         next(xy_up, None)
-        for copy in y_in:
+        gi.share_near()
+        for copy in y_in + nt:
             copy.wait_recv()
         whole = R.kvx[3, k.y].astype(F32) + sum(R.kvy[i].astype(F32) for i in range(3))
-        for n in range(3):
+        for n in range(2):
             R.kvsum[:, 128 * n:128 * n + 128] = whole[16 * n:16 * n + 16]
+        gains = R.nvt[...].astype(F32) + sum(R.nvr[i].astype(F32) for i in range(7))
+        R.kvsum[:, 256:384] = pltpu.roll(gains, (128 - 16 * k.t) % 128, axis=1)
+        next(xy_att, None)
         for xy in (xy_att, xy_up):
             for _ in xy:
                 pass
@@ -862,9 +906,9 @@
         for ag in (go, gi):
             for d in (0, 1, 3, 2):
                 ag.ready(d)
-        for copy in sent_c + sent_d + kv_in + dk_in + dk_sib + z_in + x_in + y_in + [kv_swap, sm_swap]:
+        for copy in w_x + w_y + [w_core] + sent_c + sent_d + dq_in + kv_in + dk_in + dk_sib + nx + ny + nt + x_in + y_in + [kv_swap]:
             copy.wait_send()
-        for item in (gd, rn, ou, gi, go):
+        for item in (gd, ou, gi, go):
             item.drain()
         for copy in (st_ig, st_out, kept[0], kept[1]):
             copy.wait()
@@ -901,6 +945,7 @@
     wide = ((8, 128, 2048), BF16)
     outs = [
         wide, wide, ((1024, 256), BF16), ((2624, 128), F32), ((16, 384), F32), wide, ((8, 128, 1536), BF16),
+        ((4, 2, 2, 128, 2048), BF16),
     ]
     big = b16(8, 128, 2048)
     hops = [b16(64, 2048), b16(64, 2048), b16(128, 2048), b16(128, 2048)]
@@ -911,16 +956,17 @@
         + [b16(2048, 512), b16(256, 2048), b16(1024, 256), b16(1024, 256), b16(1024, 256), b16(1024, 256)]
         + [b32(1024, 256), b32(1024, 256), b16(1024, 704), b16(1024, 704), b16(1024, 704), b32(2, 8, 2048)]
         + [b16(2, 4, 128, 256), b16(4, 128, 256), b16(3, 128, 256), b16(128, 256)]
-        + [b16(4, 4, 64, 128), b16(3, 4, 4, 16, 128), b16(4, 4, 48, 128), b16(8, 128, 256), b16(4, 4, 48, 128), b16(3, 48, 128)]
-        + [b32(128, 256), b32(2, 352, 128), pltpu.SemaphoreType.REGULAR] + [pltpu.SemaphoreType.REGULAR] * 3 + [pltpu.SemaphoreType.DMA((24,))]
+        + [b16(8, 128, 256), b16(4, 4, 32, 128), b16(3, 32, 128)]
+        + [b16(3, 4, 16, 128), b16(4, 16, 128), b16(3, 16, 128), b16(16, 128), b16(7, 16, 128)]
+        + [b32(128, 256), b32(2, 352, 128), pltpu.SemaphoreType.REGULAR] + [pltpu.SemaphoreType.REGULAR] + [pltpu.SemaphoreType.DMA((40,))]
         + [pltpu.SemaphoreType.DMA((NSEM,)), pltpu.SemaphoreType.DMA((NSEM,))]
         + grads_bufs(704) + grads_bufs(704)
     )
-    output, input_grad, shared_kv, gsum, kvsum, _, _ = pl.pallas_call(
+    output, input_grad, shared_kv, gsum, kvsum, *_ = pl.pallas_call(
         block,
         out_shape=[jax.ShapeDtypeStruct(s, d) for s, d in outs],
         in_specs=[ANY] * 10 + [VM] * 2 + [pl.BlockSpec(memory_space=pltpu.SMEM)],
-        out_specs=[ANY] * 4 + [VM] + [ANY] * 2,
+        out_specs=[ANY] * 4 + [VM] + [ANY] * 3,
         scratch_shapes=scratch,
         compiler_params=pltpu.CompilerParams(
             collective_id=0, has_side_effects=True, vmem_limit_bytes=VLIM
@@ -940,7 +986,7 @@
         compiler_params=pltpu.CompilerParams(vmem_limit_bytes=VLIM),
     )(flat(output), flat(input_grad), shared_kv, gsum)
     return (
-        output, input_grad, shared_kv, kvsum[:, 256], g_query, kvsum[:, 0:256], g_out, kvsum[:, 320],
+        output, input_grad, shared_kv, kvsum[0, 256:272], g_query, kvsum[:, 0:256], g_out, kvsum[1, 256:272],
         g_gate.T, g_up.T, g_down,
     )
 

time: 205 us -> 192 us (0.937)
  Pallas kernels: 203 us -> 190 us
    pallas_call x1, Pallas kernels: 194 us -> 181 us  [per_device(): pl.pallas_call(block, out_shape=[jax.ShapeDtypeStruct(s, d) for s, d in o...]
where the time goes in v4:
time: 192 us; the launch traced here: 191 us
  Pallas kernels  190 us (99%)
    pallas_call x1, Pallas kernels, per_device(): pl.pallas_call(block, out_shape=[jax.ShapeDtypeStruct(s, d) for s, d in o...  181 us
    pallas_call x1, Pallas kernels, per_device(): pl.pallas_call(finish, out_shape=[jax.ShapeDtypeStruct(s, d) for s, d in...  8.27 us

profile of v4, /device:TPU:1, one launch (start us, length us, event | category | flops | bytes accessed | tf_op | source)
XLA Modules:
  0.0 191.5 jit_solution(9504417534417489218)
XLA Ops:
  0.6 181.4 %shard_map.212 = (bf16[8,128,2048]{2,1,0:T(8,128)(2,1)}, bf16[8,128,2048]{2,1,0:T(8,128)(2,1)}, bf16[1024,256]{1,0:T(8,128)(2,1)}, f32[2624,128]{1,0:T(8,128)}, ...) custom-call(bf16[8,128,2048]{2,1,0:T(8,128)(2,1)} %bitcast.17, ...), custom_call_target="tpu_custom_call" | custom-call | tf_op jit(solution)/shard_map/pallas_call | solution.py:965
  182.1 0.0 copy-start
  182.1 8.3 %shard_map.213 = (bf16[1024,2048]{1,0:T(8,128)(2,1)}, bf16[1024,2048]{1,0:T(8,128)(2,1)}, bf16[1024,256]{1,0:T(8,128)(2,1)}, f32[128,256]{1,0:T(8,128)}, f32[256...) custom-call(bf16[1024,2048]{1,0:T(8,128)(2,1)} %bitcast.15, ...), custom_call_target="tpu_custom_call" | custom-call | tf_op jit(solution)/shard_map/pallas_call | solution.py:980
  190.4 0.0 copy-done
  190.4 0.5 slice_bitcast_fusion
  190.9 0.6 slice.10
Async XLA Ops:
  182.1 8.3 %copy-start = (f32[16,384]{1,0:T(8,128)S(1)}, f32[16,384]{1,0:T(8,128)}, u32[]{:S(2)}) copy-start(f32[16,384]{1,0:T(8,128)} %get-tuple-element.31) | copy-start | bytes 73732

commit v5 on v4

--- a/solution.py
+++ b/solution.py
@@ -419,29 +419,33 @@
         + [(k.dp, k.slot(d, 1 - k.c)) for d in (1, 2, 3)]
         + [dev(d) for dev in (k.xdev, k.ydev) for d in (1, 2, 3)]
     )
+    ld_cs = local(R.cs, R.csv.at[:, pl.ds(0, 128)])
     ld_q = local(R.wq, R.wqkv.at[:, pl.ds(0, 256)])
-    ld_x = local(R.x, XB)
-    ld_kv = local(R.wkv, R.wqkv.at[:, pl.ds(256, 256)])
-    ld_cs = local(R.cs, R.csv.at[:, pl.ds(0, 128)])
+    quarter = [pl.ds(2 * i, 2) for i in range(4)]
+    ld_x = [local(R.x.at[part], XB.at[part]) for part in quarter]
+    ld_cs.wait()
+    rope_rows(R.lens, R.csv)
+    ld_q.wait()
+
+    def turn_wq(i):
+        s = rows(i, 256)
+        PB[0:2, :, s] = R.wqkv[s, 0:256].T.reshape(2, 128, 256)
+
+    loop(8, turn_wq)
+    ld_ax = local(R.x.at[k.t], R.xs)
+
+    def norm1(i):
+        t, s = i // 2, rows(i % 2, 64)
+        XB[t, s] = (unit(XB[t, s].astype(F32))[0] * R.gain1[...]).astype(BF16)
+
+    for n in range(4):
+        ld_x[n].wait()
+        if n == 1:
+            ld_kv = local(R.wkv, R.wqkv.at[:, pl.ds(256, 256)])
+        loop(4, lambda i: norm1(4 * n + i))
     ld_wo = local(R.wo, R.wov)
     ld_oc = local(R.oc, OC)
     ld_ct = local(R.kvct.at[k.t], R.kvct_v)
-    ld_q.wait()
-
-    def turn_wq(i):
-        s = rows(i, 256)
-        PB[0:2, :, s] = R.wqkv[s, 0:256].T.reshape(2, 128, 256)
-
-    loop(8, turn_wq)
-
-    ld_x.wait()
-    R.xs[...] = XB[k.t]
-
-    def norm1(i):
-        t, s = i // 2, rows(i % 2, 64)
-        XB[t, s] = (unit(XB[t, s].astype(F32))[0] * R.gain1[...]).astype(BF16)
-
-    loop(16, norm1)
     st_n1 = local(XB, R.n1h)
     greeted()
     W, half = R.wall, k.y // 2
@@ -450,8 +454,6 @@
     w_z = [k.go(PB.at[half, slim], W.at[d, k.c, half, slim], k.zdev(-d)) for d in (1, 2, 3)]
     w_own = k.go(PB.at[pl.ds(0, 2)], W.at[0, k.c], k.sib())
     st_w = local(PB.at[pl.ds(0, 2)], W.at[0, k.c])
-    ld_cs.wait()
-    rope_rows(R.lens, R.csv)
     ld_kv.wait()
 
     def project(i):
@@ -521,11 +523,11 @@
     loop(4, attend)
     st_p = local(PB.at[:, :, pl.ds(0, 1536)], R.ph)
     rs.core_add(0)
-    rs.mid()
     for copy in w_x:
         copy.wait_recv()
     near = W.at[pl.ds(1, 3), k.c, half, wide]
     w_y = [k.go(near, near, k.ydev(d)) for d in (1, 2, 3)]
+    rs.mid()
     g2 = GatherZ(k, N2, N2.at[k.t])
     dn = ReduceZ(k, PA, by_turn, R.hp, R.hm, R.fp, R.fm)
     ou = ReduceZ(k, PB, by_slot, R.hp2, R.hm2, R.fp2, R.fm2)
@@ -546,6 +548,7 @@
 
         loop(4, early)
         rs.finish()
+        ld_ax.wait()
 
         def shard1(i):
             s = rows(i, 32)
@@ -599,10 +602,19 @@
             R.dg[s] = dg
             R.du[s] = du
 
+            @pl.when(d == 2)
+            def _():
+                dn.core_add(1)
+                dn.send("u1")
+                ou.core_add(1)
+                ou.send("u1")
+
             @pl.when(d == 3)
             def _():
                 dn.core_add(2)
                 dn.send("h1", "h2")
+                ou.core_add(2)
+                ou.send("h1", "h2")
 
             def cols(n):
                 w = rows(n, 512)
@@ -618,19 +630,7 @@
             @pl.when(d == 1)
             def _():
                 dn.core_add(0)
-
-            @pl.when(d == 2)
-            def _():
-                dn.core_add(1)
-                dn.send("u1")
                 ou.core_add(0)
-                ou.core_add(1)
-                ou.send("u1")
-
-            @pl.when(d == 3)
-            def _():
-                ou.core_add(2)
-                ou.send("h1", "h2")
 
         loop(4, chunk)
         dn.core_add(3)
@@ -644,10 +644,6 @@
     )
     g2.drain()
     dn.mid()
-    for copy in w_y:
-        copy.wait_recv()
-    near = W.at[pl.ds(1, 3), k.c]
-    w_core = k.go(near, near, k.sib())
 
     def weights(gm):
         sent_a, sent_b, sent_c, sent_d = [], [], [], []
@@ -679,6 +675,9 @@
         next(xy_down, None)
         ld_p = local(R.ph, OC.at[:, :, pl.ds(0, 1536)])
         ou.mid()
+        grad(R.dg, 0, 704, gm.at[1], 0, N2)
+        xy_gate = grads_xy(k, gm.at[1], bufs_b, keep(704), sent_b)
+        next(xy_gate, None)
         dn.finish()
         R.gn[...] = jnp.zeros_like(R.gn)
 
@@ -695,9 +694,10 @@
         loop(4, shard2)
         gd.start()
         dn.drain()
-        grad(R.dg, 0, 704, gm.at[1], 0, N2)
-        xy_gate = grads_xy(k, gm.at[1], bufs_b, keep(704), sent_b)
-        next(xy_gate, None)
+        for copy in w_y:
+            copy.wait_recv()
+        near = W.at[pl.ds(1, 3), k.c]
+        w_core = k.go(near, near, k.sib())
         next(xy_down, None)
         ou.finish()
 
@@ -709,22 +709,10 @@
         go = GatherZ(k, R.out, R.stage2)
         go.start()
         st_out = local(R.stage2, R.out.at[k.t])
+        grad(R.du, 0, 704, gm.at[2], 0, N2)
         gd.forward()
-        grad(R.du, 0, 704, gm.at[2], 0, N2)
         next(xy_down, None)
         next(xy_gate, None)
-        w_own.wait_recv()
-        w_core.wait_recv()
-
-        def w_block(d, c):
-            i = 2 * d + c
-            return (PA if i < 4 else N2), pl.ds(2 * (i % 4), 2)
-
-        ld_w = []
-        for d in range(4):
-            for c in range(2):
-                buf, at = w_block(d, c)
-                ld_w.append(local(W.at[d, c], buf.at[at]))
         R.dkv[...] = jnp.zeros_like(R.dkv)
         dq_in = []
 
@@ -761,21 +749,33 @@
         gd.ready(1)
         next(xy_down, None)
         next(xy_gate, None)
+        w_own.wait_recv()
+        w_core.wait_recv()
+
+        def w_block(d, c):
+            i = 2 * d + c
+            return (PA if i < 4 else N2), pl.ds(2 * (i % 4), 2)
+
+        ld_w = []
+        for d in range(4):
+            for c in range(2):
+                buf, at = w_block(d, c)
+                ld_w.append(local(W.at[d, c], buf.at[at]))
         back(1)
         for _ in xy_down:
             pass
         give(R.free_a)
         next(xy_gate, None)
+        gd.ready(3)
+        back(3)
         go.forward()
         gd.share_far()
-        gd.ready(2)
-        back(2)
         pl.semaphore_wait(R.free_a, 4)
         xy_up = grads_xy(k, gm.at[2], bufs_a, keep(1408), sent_c)
         next(xy_up, None)
+        gd.ready(2)
+        back(2)
         go.share_near()
-        gd.ready(3)
-        back(3)
         for d in range(4):
             for c in range(2):
                 R.kvb[c, d] = R.dkv[(2 * d + c) * 128:(2 * d + c) * 128 + 128].astype(BF16)
@@ -857,9 +857,9 @@
             copy.wait_recv()
         theirs = [dkw.at[rows(k.slot(d), 128)] for d in (1, 2, 3)]
         dk_sib += [k.go(piece, piece, k.sib()) for piece in theirs]
-        go.share_far()
         next(xy_att, None)
         next(xy_up, None)
+        go.share_far()
         for copy in nx:
             copy.wait_recv()
         R.nvs[...] = (sm[k.x, :, line].astype(F32) + sum(R.nvx[i].astype(F32) for i in range(3))).astype(BF16)

time: 192 us -> 191 us (level)
  no operation moved by 1% of the time
where the time goes in v5:
time: 191 us
  Pallas kernels  189 us (99%)
    pallas_call x1, Pallas kernels, per_device(): pl.pallas_call(block, out_shape=[jax.ShapeDtypeStruct(s, d) for s, d in o...  181 us
    pallas_call x1, Pallas kernels, per_device(): pl.pallas_call(finish, out_shape=[jax.ShapeDtypeStruct(s, d) for s, d in...  8.27 us

profile of v5, /device:TPU:1, one launch (start us, length us, event | category | flops | bytes accessed | tf_op | source)
XLA Modules:
  0.0 191.3 jit_solution(16994511390504511269)
XLA Ops:
  0.6 181.2 %shard_map.212 = (bf16[8,128,2048]{2,1,0:T(8,128)(2,1)}, bf16[8,128,2048]{2,1,0:T(8,128)(2,1)}, bf16[1024,256]{1,0:T(8,128)(2,1)}, f32[2624,128]{1,0:T(8,128)}, ...) custom-call(bf16[8,128,2048]{2,1,0:T(8,128)(2,1)} %bitcast.17, ...), custom_call_target="tpu_custom_call" | custom-call | tf_op jit(solution)/shard_map/pallas_call | solution.py:965
  181.8 0.0 copy-start
  181.8 8.3 %shard_map.213 = (bf16[1024,2048]{1,0:T(8,128)(2,1)}, bf16[1024,2048]{1,0:T(8,128)(2,1)}, bf16[1024,256]{1,0:T(8,128)(2,1)}, f32[128,256]{1,0:T(8,128)}, f32[256...) custom-call(bf16[1024,2048]{1,0:T(8,128)(2,1)} %bitcast.15, ...), custom_call_target="tpu_custom_call" | custom-call | tf_op jit(solution)/shard_map/pallas_call | solution.py:980
  190.1 0.0 copy-done
  190.1 0.5 slice_bitcast_fusion
  190.7 0.6 slice.10
Async XLA Ops:
  181.8 8.3 %copy-start = (f32[16,384]{1,0:T(8,128)S(1)}, f32[16,384]{1,0:T(8,128)}, u32[]{:S(2)}) copy-start(f32[16,384]{1,0:T(8,128)} %get-tuple-element.31) | copy-start | bytes 73732
